TPU v7x, 32 devices: a whole 2x2x4 slice. The times are simulated.
32 devices in a mesh: groups: 2 (over y), tile: 16 (over z, x, core).
Axes of the slice: x: 2, y: 2, z: 4, core: 2. Of those that a mesh axis runs over, the one named last changes fastest.
Arguments:
- level_map: int32 [16], replicated, may hold values from 0 to 7, as said below
- loc_lat: bfloat16 [256, 256], replicated, may hold values from -0.1875 to 0.1875
- loc_lon: bfloat16 [256, 256], replicated, may hold values from -0.1875 to 0.1875
- ens_perts: bfloat16 [32, 256, 256], P(('groups', 'tile')), parts along dimension 0, may hold values from -4 to 4
- ens_control: float32 [32, 256, 256], P(('groups', 'tile')), parts along dimension 0, may hold values from -6 to 6
- static_control: float32 [16, 256, 256], P('groups', 'tile'), parts along dimension 0, may hold values from -6 to 6
- static_scale: float32 [16, 256, 256], P('groups', 'tile'), parts along dimension 0, may hold values from 0.3 to 1.5
- coefs: float32 [4, 16, 256, 256], P(None, 'groups', 'tile'), parts along dimension 1, may hold values from 0.02 to 0.24
- obs_weight: float32 [3, 16, 256, 256], P(None, 'groups', 'tile'), parts along dimension 1, may hold values from 0.05 to 0.5
- innovation: float32 [3, 16, 256, 256], P(None, 'groups', 'tile'), parts along dimension 1, may hold values from -6 to 6
Outputs:
- ens_final: float32 [32, 256, 256], P(('groups', 'tile')), parts along dimension 0
- static_final: float32 [16, 256, 256], P('groups', 'tile'), parts along dimension 0
There are 2 independent parts, one for each index of `groups`. A program takes and returns all parts, laid end to end along the dimension named above; an argument that names none is the same for every part. Nothing has to cross between parts.
Inputs may be any that keep to these rules, and one draw needn't show every extreme that they name: `level_map`: each of the 8 levels is named by exactly 2 entries.
All inputs are finite; a program needn't handle non-finite values.
Results may differ from a plain program's by a relative error of at most 0.0003.
Values sent between devices are 32-bit elements; how exact they have to be, the bound alone decides.
A program may use at most 64 MiB of HBM per device.

v0:
```python
import jax
import jax.numpy as jnp
from jax import lax
from jax.sharding import PartitionSpec as P

STEPS = 3


step_size = 0.15


def extended(block, sides, width):
    for axis, dim in sides:
        count = lax.axis_size(axis)
        forward = [(i, i + 1) for i in range(count - 1)]
        backward = [(target, source) for source, target in forward]
        low = lax.ppermute(
            lax.slice_in_dim(block, block.shape[dim] - width, None, axis=dim), axis, forward
        )
        high = lax.ppermute(lax.slice_in_dim(block, 0, width, axis=dim), axis, backward)
        block = jnp.concatenate([low, block, high], axis=dim)
    return block


def forward_step(state, coeffs):
    padded = extended(state, (("tile", 1),), 1)
    north_rows = padded[:, 2:]
    south_rows = padded[:, :-2]
    east_cells = jnp.roll(state, -1, 2)
    west_cells = jnp.roll(state, 1, 2)
    return (
        state
        + coeffs[0] * (north_rows - state)
        + coeffs[1] * (south_rows - state)
        + coeffs[2] * (east_cells - state)
        + coeffs[3] * (west_cells - state)
    )


def adjoint_step(adjoint, coeffs):
    coef_sum = coeffs[0] + coeffs[1] + coeffs[2] + coeffs[3]
    fluxes = jnp.stack([coeffs[0] * adjoint, coeffs[1] * adjoint])
    padded = extended(fluxes, (("tile", 2),), 1)
    north_flux = padded[0][:, :-2]
    south_flux = padded[1][:, 2:]
    return (
        (1.0 - coef_sum) * adjoint
        + north_flux
        + south_flux
        + jnp.roll(coeffs[2] * adjoint, 1, 2)
        + jnp.roll(coeffs[3] * adjoint, -1, 2)
    )


def window_gradient(total_incr, coefs, obs_weight, innovation):
    state = total_incr
    weighted = []
    for section in range(STEPS):
        state = forward_step(state, coefs)
        weighted.append(obs_weight[section] * (state - innovation[section]))
    adjoint = weighted[STEPS - 1]
    for section in range(STEPS - 2, -1, -1):
        adjoint = adjoint_step(adjoint, coefs) + weighted[section]
    return adjoint_step(adjoint, coefs)


def local(
    level_map,
    loc_lat,
    loc_lon,
    ens_perts,
    ens_control,
    static_control,
    static_scale,
    coefs,
    obs_weight,
    innovation,
):
    tile_count = lax.axis_size("tile")
    my_level = level_map[lax.axis_index("tile")]
    levels = static_control.shape[0]
    level_ids = jnp.arange(levels, dtype=jnp.int32)
    level_onehot = (level_map[:, None] == level_ids[None, :]).astype(jnp.float32)
    control = ens_control
    lat_smoothed = jnp.einsum(
        "ij,bjk->bik", loc_lat, control.astype(jnp.bfloat16), preferred_element_type=jnp.float32
    ).astype(jnp.bfloat16)
    member_field = jnp.einsum(
        "bij,kj->bik", lat_smoothed, loc_lon, preferred_element_type=jnp.float32
    )
    partial_value = jnp.sum(ens_perts.astype(jnp.float32) * member_field, axis=0)
    pieces = partial_value.reshape(tile_count, -1, partial_value.shape[1])
    received = lax.all_to_all(pieces, "tile", split_axis=0, concat_axis=0, tiled=True)
    ens_incr = jnp.einsum("dl,dij->lij", level_onehot, received, precision=lax.Precision.HIGHEST)
    total_incr = static_scale * static_control + ens_incr
    gradient = window_gradient(total_incr, coefs, obs_weight, innovation)
    static_control = static_control - step_size * (static_control + static_scale * gradient)
    gathered = lax.all_gather(gradient, "tile", axis=1, tiled=True)
    grad_field = lax.dynamic_index_in_dim(gathered, my_level, 0, keepdims=False)
    weighted_grad = (ens_perts.astype(jnp.float32) * grad_field[None]).astype(jnp.bfloat16)
    adjoint_lat = jnp.einsum(
        "ji,bjk->bik", loc_lat, weighted_grad, preferred_element_type=jnp.float32
    ).astype(jnp.bfloat16)
    member_grad = jnp.einsum(
        "bij,jk->bik", adjoint_lat, loc_lon, preferred_element_type=jnp.float32
    )
    control = control - step_size * (control + member_grad)
    return (control, static_control)


def solution(mesh):
    in_specs = (
        P(),
        P(),
        P(),
        P(("groups", "tile"), None, None),
        P(("groups", "tile"), None, None),
        P("groups", "tile", None),
        P("groups", "tile", None),
        P(None, "groups", "tile", None),
        P(None, "groups", "tile", None),
        P(None, "groups", "tile", None),
    )
    out_specs = (P(("groups", "tile"), None, None), P("groups", "tile", None))
    return jax.shard_map(local, mesh=mesh, in_specs=in_specs, out_specs=out_specs, check_vma=False)
```

profile of v0, /device:TPU:0, one launch (start us, length us, event | category | flops | bytes accessed | tf_op | source)
XLA Modules:
  0.0 129.2 jit_solution(13692890221290343578)
XLA Ops:
  7.2 0.0 all-gather.2.cloned.1.call-start
  7.2 0.8 copy-done
  8.1 1.5 %fusion = f32[1,256,256]{2,1,0:T(8,128)S(1)} fusion(bf16[256,256]{1,0:T(8,128)(2,1)S(1)} %copy-done, bf16[256,256]{1,0:T(8,128)(2,1)} %param.11, bf16[1,256,256]{2,1,0:T(8,128)(2,1)} %param.13, f32[1,256,256]{2,1,0:T(8,128)} %param.14), kind=kOutput, calls=%fused_computation.2 | convolution fusion | flops 67371008 | bytes 917504 | tf_op jit(solution)/shard_map/bij,kj->bik/dot_general | solution.py:88
  9.6 17.2 %all_to_all.5 = f32[16,16,256]{2,1,0:T(8,128)S(1)} all-to-all(f32[16,16,256]{2,1,0:T(8,128)S(1)} %bitcast.156), channel_id=1, replica_groups=mesh['groups'=2,'tile'=16] {'tile'}, dimensions={0} | all-to-all | bytes 524288 | tf_op jit(solution)/shard_map/all_to_all | solution.py:93
  26.8 1.0 fusion.7
  27.8 1.0 copy_add_fusion
  28.9 0.1 fusion.82
  29.0 1.3 %collective-permute-start = (f32[8,1,256]{2,1,0:T(1,128)S(1)}, f32[8,1,256]{2,1,0:T(1,128)S(1)}, u32[]{:S(2)}, u32[]{:S(2)}) collective-permute-start(f32[8,1,256]{2,1,0:T(1,128)S(1)} %get-tuple-element.48), channel_id=1, source_target_pairs={{1,0},{2,1},{3,2},{4,3},{5,4},{6,5},{7,6},{8,7},{9,8},{10,9},{11,1... | collective-permute-start | bytes 24584 | tf_op jit(solution)/shard_map/ppermute | solution.py:20
  30.3 3.2 %collective-permute-start.1 = (f32[8,1,256]{2,1,0:T(1,128)S(1)}, f32[8,1,256]{2,1,0:T(1,128)S(1)}, u32[]{:S(2)}, u32[]{:S(2)}) collective-permute-start(f32[8,1,256]{2,1,0:T(1,128)S(1)} %get-tuple-element.49), channel_id=1, source_target_pairs={{0,1},{1,2},{2,3},{3,4},{4,5},{5,6},{6,7},{7,8},{8,9},{9,10},{10,1... | collective-permute-start | bytes 24584 | tf_op jit(solution)/shard_map/ppermute | solution.py:17
  33.5 0.1 fusion.81
  33.6 0.7 collective-permute-done.1
  34.3 0.1 fusion.42
  34.4 0.1 fusion.79
  34.5 1.3 %collective-permute-start.2 = (f32[8,1,256]{2,1,0:T(1,128)S(1)}, f32[8,1,256]{2,1,0:T(1,128)S(1)}, u32[]{:S(2)}, u32[]{:S(2)}) collective-permute-start(f32[8,1,256]{2,1,0:T(1,128)S(1)} %get-tuple-element.42), channel_id=1, source_target_pairs={{1,0},{2,1},{3,2},{4,3},{5,4},{6,5},{7,6},{8,7},{9,8},{10,9},{11,1... | collective-permute-start | bytes 24584 | tf_op jit(solution)/shard_map/ppermute | solution.py:20
  35.8 3.6 %collective-permute-start.3 = (f32[8,1,256]{2,1,0:T(1,128)S(1)}, f32[8,1,256]{2,1,0:T(1,128)S(1)}, u32[]{:S(2)}, u32[]{:S(2)}) collective-permute-start(f32[8,1,256]{2,1,0:T(1,128)S(1)} %get-tuple-element.43), channel_id=1, source_target_pairs={{0,1},{1,2},{2,3},{3,4},{4,5},{5,6},{6,7},{7,8},{8,9},{9,10},{10,1... | collective-permute-start | bytes 24584 | tf_op jit(solution)/shard_map/ppermute | solution.py:17
  39.4 0.1 fusion.78
  39.5 0.7 collective-permute-done.3
  40.2 0.1 fusion.34
  40.4 0.1 fusion.76
  40.5 1.3 %collective-permute-start.4 = (f32[8,1,256]{2,1,0:T(1,128)S(1)}, f32[8,1,256]{2,1,0:T(1,128)S(1)}, u32[]{:S(2)}, u32[]{:S(2)}) collective-permute-start(f32[8,1,256]{2,1,0:T(1,128)S(1)} %get-tuple-element.32), channel_id=1, source_target_pairs={{1,0},{2,1},{3,2},{4,3},{5,4},{6,5},{7,6},{8,7},{9,8},{10,9},{11,1... | collective-permute-start | bytes 24584 | tf_op jit(solution)/shard_map/ppermute | solution.py:20
  41.8 4.8 %collective-permute-start.5 = (f32[8,1,256]{2,1,0:T(1,128)S(1)}, f32[8,1,256]{2,1,0:T(1,128)S(1)}, u32[]{:S(2)}, u32[]{:S(2)}) collective-permute-start(f32[8,1,256]{2,1,0:T(1,128)S(1)} %get-tuple-element.33), channel_id=1, source_target_pairs={{0,1},{1,2},{2,3},{3,4},{4,5},{5,6},{6,7},{7,8},{8,9},{9,10},{10,1... | collective-permute-start | bytes 24584 | tf_op jit(solution)/shard_map/ppermute | solution.py:17
  46.6 0.1 fusion.77
  46.7 0.7 collective-permute-done.5
  47.4 0.1 bitcast_multiply_fusion.2
  47.6 4.2 %collective-permute-start.6 = (f32[2,8,1,256]{3,2,1,0:T(1,128)S(1)}, f32[2,8,1,256]{3,2,1,0:T(1,128)S(1)}, u32[]{:S(2)}, u32[]{:S(2)}) collective-permute-start(f32[2,8,1,256]{3,2,1,0:T(1,128)S(1)} %get-tuple-element.30), channel_id=1, source_target_pairs={{0,1},{1,2},{2,3},{3,4},{4,5},{5,6},{6,7},{7,8},{8,9},{9,10},{10,1... | collective-permute-start | bytes 49160 | tf_op jit(solution)/shard_map/ppermute | solution.py:17
  51.8 1.3 %collective-permute-start.7 = (f32[2,8,1,256]{3,2,1,0:T(1,128)S(1)}, f32[2,8,1,256]{3,2,1,0:T(1,128)S(1)}, u32[]{:S(2)}, u32[]{:S(2)}) collective-permute-start(f32[2,8,1,256]{3,2,1,0:T(1,128)S(1)} %get-tuple-element.31), channel_id=1, source_target_pairs={{1,0},{2,1},{3,2},{4,3},{5,4},{6,5},{7,6},{8,7},{9,8},{10,9},{11,1... | collective-permute-start | bytes 49160 | tf_op jit(solution)/shard_map/ppermute | solution.py:20
  53.1 0.1 slice.322
  53.2 0.1 slice.320
  53.3 3.4 %collective-permute-done.7 = f32[2,8,1,256]{3,2,1,0:T(1,128)S(1)} collective-permute-done((f32[2,8,1,256]{3,2,1,0:T(1,128)S(1)}, f32[2,8,1,256]{3,2,1,0:T(1,128)S(1)}, u32[]{:S(2)}, u32[]{:S(2)}) %collective-permute-start.7) | collective-permute-done | bytes 16416 | tf_op jit(solution)/shard_map/ppermute | solution.py:20
  56.7 0.1 pad_maximum_fusion
  56.8 0.2 bitcast_multiply_fusion.1
  57.0 4.4 %collective-permute-start.8 = (f32[2,8,1,256]{3,2,1,0:T(1,128)S(1)}, f32[2,8,1,256]{3,2,1,0:T(1,128)S(1)}, u32[]{:S(2)}, u32[]{:S(2)}) collective-permute-start(f32[2,8,1,256]{3,2,1,0:T(1,128)S(1)} %get-tuple-element.28), channel_id=1, source_target_pairs={{0,1},{1,2},{2,3},{3,4},{4,5},{5,6},{6,7},{7,8},{8,9},{9,10},{10,1... | collective-permute-start | bytes 49160 | tf_op jit(solution)/shard_map/ppermute | solution.py:17
  61.4 1.3 %collective-permute-start.9 = (f32[2,8,1,256]{3,2,1,0:T(1,128)S(1)}, f32[2,8,1,256]{3,2,1,0:T(1,128)S(1)}, u32[]{:S(2)}, u32[]{:S(2)}) collective-permute-start(f32[2,8,1,256]{3,2,1,0:T(1,128)S(1)} %get-tuple-element.29), channel_id=1, source_target_pairs={{1,0},{2,1},{3,2},{4,3},{5,4},{6,5},{7,6},{8,7},{9,8},{10,9},{11,1... | collective-permute-start | bytes 49160 | tf_op jit(solution)/shard_map/ppermute | solution.py:20
  62.7 0.1 slice.330
  62.8 0.1 slice.328
  62.9 3.0 %collective-permute-done.9 = f32[2,8,1,256]{3,2,1,0:T(1,128)S(1)} collective-permute-done((f32[2,8,1,256]{3,2,1,0:T(1,128)S(1)}, f32[2,8,1,256]{3,2,1,0:T(1,128)S(1)}, u32[]{:S(2)}, u32[]{:S(2)}) %collective-permute-start.9) | collective-permute-done | bytes 16416 | tf_op jit(solution)/shard_map/ppermute | solution.py:20
  65.9 0.1 pad_maximum_fusion.1
  66.0 0.2 bitcast_multiply_fusion
  66.3 6.2 %collective-permute-start.10 = (f32[2,8,1,256]{3,2,1,0:T(1,128)S(1)}, f32[2,8,1,256]{3,2,1,0:T(1,128)S(1)}, u32[]{:S(2)}, u32[]{:S(2)}) collective-permute-start(f32[2,8,1,256]{3,2,1,0:T(1,128)S(1)} %get-tuple-element.26), channel_id=1, source_target_pairs={{0,1},{1,2},{2,3},{3,4},{4,5},{5,6},{6,7},{7,8},{8,9},{9,10},{10,1... | collective-permute-start | bytes 49160 | tf_op jit(solution)/shard_map/ppermute | solution.py:17
  72.5 1.3 %collective-permute-start.11 = (f32[2,8,1,256]{3,2,1,0:T(1,128)S(1)}, f32[2,8,1,256]{3,2,1,0:T(1,128)S(1)}, u32[]{:S(2)}, u32[]{:S(2)}) collective-permute-start(f32[2,8,1,256]{3,2,1,0:T(1,128)S(1)} %get-tuple-element.27), channel_id=1, source_target_pairs={{1,0},{2,1},{3,2},{4,3},{5,4},{6,5},{7,6},{8,7},{9,8},{10,9},{11,1... | collective-permute-start | bytes 49160 | tf_op jit(solution)/shard_map/ppermute | solution.py:20
  73.8 0.1 slice.338
  73.9 0.1 slice.336
  74.0 1.6 %collective-permute-done.11 = f32[2,8,1,256]{3,2,1,0:T(1,128)S(1)} collective-permute-done((f32[2,8,1,256]{3,2,1,0:T(1,128)S(1)}, f32[2,8,1,256]{3,2,1,0:T(1,128)S(1)}, u32[]{:S(2)}, u32[]{:S(2)}) %collective-permute-start.11) | collective-permute-done | bytes 16416 | tf_op jit(solution)/shard_map/ppermute | solution.py:20
  75.6 0.1 pad_maximum_fusion.2
  75.7 0.8 multiply_subtract_fusion
  76.5 0.6 dynamic_slice.7
  79.0 41.2 %all-gather.2.cloned.1.call-done = f32[8,256,256]{2,1,0:T(8,128)} async-done(((f32[8,16,256]{2,1,0:T(8,128)}), f32[8,256,256]{2,1,0:T(8,128)}) %all-gather.2.cloned.1.call-update) | async-done | bytes 2097168 | tf_op jit(solution)/shard_map/all_gather | solution.py:98
  120.2 2.1 %fusion.3 = f32[1,256,256]{2,1,0:T(8,128)} fusion(f32[1,256,256]{2,1,0:T(8,128)S(1)} %copy-done.2, bf16[256,256]{1,0:T(8,128)(2,1)S(1)} %copy-done, bf16[256,256]{1,0:T(8,128)(2,1)S(1)} %copy-done.3, f32[8,256,256]{2,1,0:T(8,128)} %all-gather.2.cloned.1.call-done, s32[]{:T(128)S(6)} %select_n.8, bf16[1,256,256]{2,1,0:T(8,128)(2,1)S(1)} %copy-done.4), kind=kOutput, calls=%fused_computation.5 | convolution fusion | flops 67567616 | bytes 1179652 | tf_op jit(solution)/shard_map/bij,jk->bik/dot_general | solution.py:104
  (41 shorter events, 0.4 us)
Async XLA Ops:
  7.2 0.9 copy-start
  7.2 27.1 %copy-start.1 = (f32[4,8,16,256]{3,2,1,0:T(8,128)S(1)}, f32[4,8,16,256]{3,2,1,0:T(8,128)}, u32[]{:S(2)}) copy-start(f32[4,8,16,256]{3,2,1,0:T(8,128)} %param.17) | copy-start | bytes 1572868
  7.2 113.0 %all-gather.2.cloned.1.call-start = ((), (), s32[]{:S(2)}) async-start(), calls=%async_computation.1 | async-start | bytes 2228224 | tf_op jit(solution)/shard_map/all_gather | solution.py:98
  29.0 4.6 %collective-permute-start = (f32[8,1,256]{2,1,0:T(1,128)S(1)}, f32[8,1,256]{2,1,0:T(1,128)S(1)}, u32[]{:S(2)}, u32[]{:S(2)}) collective-permute-start(f32[8,1,256]{2,1,0:T(1,128)S(1)} %get-tuple-element.48), channel_id=1, source_target_pairs={{1,0},{2,1},{3,2},{4,3},{5,4},{6,5},{7,6},{8,7},{9,8},{10,9},{11,1... | collective-permute-start | bytes 24584 | tf_op jit(solution)/shard_map/ppermute | solution.py:20
  30.3 17.1 %copy-start.7 = (f32[3,8,16,256]{3,2,1,0:T(8,128)S(1)}, f32[3,8,16,256]{3,2,1,0:T(8,128)}, u32[]{:S(2)}) copy-start(f32[3,8,16,256]{3,2,1,0:T(8,128)} %param.19) | copy-start | bytes 1179652
  30.3 17.1 %copy-start.8 = (f32[3,8,16,256]{3,2,1,0:T(8,128)S(1)}, f32[3,8,16,256]{3,2,1,0:T(8,128)}, u32[]{:S(2)}) copy-start(f32[3,8,16,256]{3,2,1,0:T(8,128)} %param.18) | copy-start | bytes 1179652
  30.3 4.0 %collective-permute-start.1 = (f32[8,1,256]{2,1,0:T(1,128)S(1)}, f32[8,1,256]{2,1,0:T(1,128)S(1)}, u32[]{:S(2)}, u32[]{:S(2)}) collective-permute-start(f32[8,1,256]{2,1,0:T(1,128)S(1)} %get-tuple-element.49), channel_id=1, source_target_pairs={{0,1},{1,2},{2,3},{3,4},{4,5},{5,6},{6,7},{7,8},{8,9},{9,10},{10,1... | collective-permute-start | bytes 24584 | tf_op jit(solution)/shard_map/ppermute | solution.py:17
  34.5 5.0 %collective-permute-start.2 = (f32[8,1,256]{2,1,0:T(1,128)S(1)}, f32[8,1,256]{2,1,0:T(1,128)S(1)}, u32[]{:S(2)}, u32[]{:S(2)}) collective-permute-start(f32[8,1,256]{2,1,0:T(1,128)S(1)} %get-tuple-element.42), channel_id=1, source_target_pairs={{1,0},{2,1},{3,2},{4,3},{5,4},{6,5},{7,6},{8,7},{9,8},{10,9},{11,1... | collective-permute-start | bytes 24584 | tf_op jit(solution)/shard_map/ppermute | solution.py:20
  35.8 4.4 %collective-permute-start.3 = (f32[8,1,256]{2,1,0:T(1,128)S(1)}, f32[8,1,256]{2,1,0:T(1,128)S(1)}, u32[]{:S(2)}, u32[]{:S(2)}) collective-permute-start(f32[8,1,256]{2,1,0:T(1,128)S(1)} %get-tuple-element.43), channel_id=1, source_target_pairs={{0,1},{1,2},{2,3},{3,4},{4,5},{5,6},{6,7},{7,8},{8,9},{9,10},{10,1... | collective-permute-start | bytes 24584 | tf_op jit(solution)/shard_map/ppermute | solution.py:17
  40.5 6.2 %collective-permute-start.4 = (f32[8,1,256]{2,1,0:T(1,128)S(1)}, f32[8,1,256]{2,1,0:T(1,128)S(1)}, u32[]{:S(2)}, u32[]{:S(2)}) collective-permute-start(f32[8,1,256]{2,1,0:T(1,128)S(1)} %get-tuple-element.32), channel_id=1, source_target_pairs={{1,0},{2,1},{3,2},{4,3},{5,4},{6,5},{7,6},{8,7},{9,8},{10,9},{11,1... | collective-permute-start | bytes 24584 | tf_op jit(solution)/shard_map/ppermute | solution.py:20
  41.8 5.6 %collective-permute-start.5 = (f32[8,1,256]{2,1,0:T(1,128)S(1)}, f32[8,1,256]{2,1,0:T(1,128)S(1)}, u32[]{:S(2)}, u32[]{:S(2)}) collective-permute-start(f32[8,1,256]{2,1,0:T(1,128)S(1)} %get-tuple-element.33), channel_id=1, source_target_pairs={{0,1},{1,2},{2,3},{3,4},{4,5},{5,6},{6,7},{7,8},{8,9},{9,10},{10,1... | collective-permute-start | bytes 24584 | tf_op jit(solution)/shard_map/ppermute | solution.py:17
  47.6 5.7 %collective-permute-start.6 = (f32[2,8,1,256]{3,2,1,0:T(1,128)S(1)}, f32[2,8,1,256]{3,2,1,0:T(1,128)S(1)}, u32[]{:S(2)}, u32[]{:S(2)}) collective-permute-start(f32[2,8,1,256]{3,2,1,0:T(1,128)S(1)} %get-tuple-element.30), channel_id=1, source_target_pairs={{0,1},{1,2},{2,3},{3,4},{4,5},{5,6},{6,7},{7,8},{8,9},{9,10},{10,1... | collective-permute-start | bytes 49160 | tf_op jit(solution)/shard_map/ppermute | solution.py:17
  51.8 4.9 %collective-permute-start.7 = (f32[2,8,1,256]{3,2,1,0:T(1,128)S(1)}, f32[2,8,1,256]{3,2,1,0:T(1,128)S(1)}, u32[]{:S(2)}, u32[]{:S(2)}) collective-permute-start(f32[2,8,1,256]{3,2,1,0:T(1,128)S(1)} %get-tuple-element.31), channel_id=1, source_target_pairs={{1,0},{2,1},{3,2},{4,3},{5,4},{6,5},{7,6},{8,7},{9,8},{10,9},{11,1... | collective-permute-start | bytes 49160 | tf_op jit(solution)/shard_map/ppermute | solution.py:20
  57.0 5.9 %collective-permute-start.8 = (f32[2,8,1,256]{3,2,1,0:T(1,128)S(1)}, f32[2,8,1,256]{3,2,1,0:T(1,128)S(1)}, u32[]{:S(2)}, u32[]{:S(2)}) collective-permute-start(f32[2,8,1,256]{3,2,1,0:T(1,128)S(1)} %get-tuple-element.28), channel_id=1, source_target_pairs={{0,1},{1,2},{2,3},{3,4},{4,5},{5,6},{6,7},{7,8},{8,9},{9,10},{10,1... | collective-permute-start | bytes 49160 | tf_op jit(solution)/shard_map/ppermute | solution.py:17
  61.4 4.5 %collective-permute-start.9 = (f32[2,8,1,256]{3,2,1,0:T(1,128)S(1)}, f32[2,8,1,256]{3,2,1,0:T(1,128)S(1)}, u32[]{:S(2)}, u32[]{:S(2)}) collective-permute-start(f32[2,8,1,256]{3,2,1,0:T(1,128)S(1)} %get-tuple-element.29), channel_id=1, source_target_pairs={{1,0},{2,1},{3,2},{4,3},{5,4},{6,5},{7,6},{8,7},{9,8},{10,9},{11,1... | collective-permute-start | bytes 49160 | tf_op jit(solution)/shard_map/ppermute | solution.py:20
  66.0 9.7 %copy-start.5 = (f32[8,16,256]{2,1,0:T(8,128)S(1)}, f32[8,16,256]{2,1,0:T(8,128)}, u32[]{:S(2)}) copy-start(f32[8,16,256]{2,1,0:T(8,128)} %param.15) | copy-start | bytes 393220
  66.0 9.7 %copy-start.6 = (f32[8,16,256]{2,1,0:T(8,128)S(1)}, f32[8,16,256]{2,1,0:T(8,128)}, u32[]{:S(2)}) copy-start(f32[8,16,256]{2,1,0:T(8,128)} %param.16) | copy-start | bytes 393220
  66.2 10.3 %copy-start.9 = (s32[16]{0:T(128)S(1)}, s32[16]{0:T(128)}, u32[]{:S(2)}) copy-start(s32[16]{0:T(128)} %param.10) | copy-start | bytes 196
  66.3 54.0 %copy-start.2 = (f32[1,256,256]{2,1,0:T(8,128)S(1)}, f32[1,256,256]{2,1,0:T(8,128)}, u32[]{:S(2)}) copy-start(f32[1,256,256]{2,1,0:T(8,128)} %param.14) | copy-start | bytes 786436
  66.3 54.0 %copy-start.3 = (bf16[256,256]{1,0:T(8,128)(2,1)S(1)}, bf16[256,256]{1,0:T(8,128)(2,1)}, u32[]{:S(2)}) copy-start(bf16[256,256]{1,0:T(8,128)(2,1)} %param.11) | copy-start | bytes 393220
  66.3 53.9 %copy-start.4 = (bf16[1,256,256]{2,1,0:T(8,128)(2,1)S(1)}, bf16[1,256,256]{2,1,0:T(8,128)(2,1)}, u32[]{:S(2)}) copy-start(bf16[1,256,256]{2,1,0:T(8,128)(2,1)} %param.13) | copy-start | bytes 393220
  66.3 7.7 %collective-permute-start.10 = (f32[2,8,1,256]{3,2,1,0:T(1,128)S(1)}, f32[2,8,1,256]{3,2,1,0:T(1,128)S(1)}, u32[]{:S(2)}, u32[]{:S(2)}) collective-permute-start(f32[2,8,1,256]{3,2,1,0:T(1,128)S(1)} %get-tuple-element.26), channel_id=1, source_target_pairs={{0,1},{1,2},{2,3},{3,4},{4,5},{5,6},{6,7},{7,8},{8,9},{9,10},{10,1... | collective-permute-start | bytes 49160 | tf_op jit(solution)/shard_map/ppermute | solution.py:17
  72.5 3.1 %collective-permute-start.11 = (f32[2,8,1,256]{3,2,1,0:T(1,128)S(1)}, f32[2,8,1,256]{3,2,1,0:T(1,128)S(1)}, u32[]{:S(2)}, u32[]{:S(2)}) collective-permute-start(f32[2,8,1,256]{3,2,1,0:T(1,128)S(1)} %get-tuple-element.27), channel_id=1, source_target_pairs={{1,0},{2,1},{3,2},{4,3},{5,4},{6,5},{7,6},{8,7},{9,8},{10,9},{11,1... | collective-permute-start | bytes 49160 | tf_op jit(solution)/shard_map/ppermute | solution.py:20
Sparse Core Ops, SparseCore 0:
  76.7 43.5 all-gather.1
where the time goes:
time: 130 us; the launch traced here: 129 us
  waiting for transfers between devices  51.4 us (40%)
  starting transfers between devices  34 us (26%)
  blocking collectives  17.2 us (13%)
  between operations  16.3 us (13%)
  matrix products  4.64 us (4%)
  other arithmetic  2.97 us (2%)
  local copies, waits for them, and re-layouts  2.66 us (2%)
    all_gather x1, waiting for transfers between devices, local(): gathered = lax.all_gather(gradient, 'tile', axis=1, tiled=True)  41.2 us
    ppermute x6, starting transfers between devices, extended(): lax.ppermute(lax.slice_in_dim(block, block.shape[dim] - width, None, axis...  26.2 us
    all_to_all x1, blocking collectives, local(): lax.all_to_all(pieces, 'tile', split_axis=0, concat_axis=0, tiled=True)  17.2 us
    ppermute x6, waiting for transfers between devices, extended(): lax.ppermute(lax.slice_in_dim(block, 0, width, axis=dim), axis, backward)  7.93 us
    ppermute x6, starting transfers between devices, extended(): lax.ppermute(lax.slice_in_dim(block, 0, width, axis=dim), axis, backward)  7.75 us
  transfers between devices with their start and end apart: 13, of which 7 were waited for; matrix products, arithmetic and copies ran while one was open for 1% of the time, Pallas kernels for 0%

commit v1 on v0

--- a/solution.py
+++ b/solution.py
@@ -1,6 +1,10 @@
+import functools
+
 import jax
 import jax.numpy as jnp
 from jax import lax
+from jax.experimental import pallas as pl
+from jax.experimental.pallas import tpu as pltpu
 from jax.sharding import PartitionSpec as P
 
 STEPS = 3
@@ -108,6 +112,374 @@
     return (control, static_control)
 
 
+MESH = pl.DeviceIdType.MESH
+SIDE = 4
+
+
+def kernel(
+    n,
+    level_map,
+    lat_hbm,
+    lon_hbm,
+    perts_hbm,
+    control_hbm,
+    static_hbm,
+    scale_hbm,
+    coefs_hbm,
+    weight_hbm,
+    innov_hbm,
+    ens_out,
+    static_out,
+    lat,
+    lon,
+    perts,
+    control,
+    static,
+    scale,
+    coefs,
+    weight,
+    innov,
+    lat_t,
+    field,
+    received,
+    coef_win,
+    keep_win,
+    total_win,
+    weight_win,
+    innov_win,
+    weighted,
+    early_send,
+    early_recv,
+    late_send,
+    late_recv,
+    grad,
+    grad_send,
+    grad_field,
+    ens_new,
+    static_new,
+    in_sem,
+    out_sem,
+    member_send_sem,
+    member_recv_sem,
+    early_send_sem,
+    early_recv_sem,
+    late_send_sem,
+    late_recv_sem,
+    grad_send_sem,
+    grad_recv_sem,
+):
+    me = lax.axis_index("tile")
+    levels, rows, cols = static.shape
+    nlat = control.shape[0]
+    win = rows + 2 * SIDE
+    main = slice(SIDE, SIDE + rows)
+
+    loads = {}
+    for place, (name, source, target) in enumerate(
+        (
+            ("control", control_hbm.at[0], control),
+            ("lat", lat_hbm, lat),
+            ("lon", lon_hbm, lon),
+            ("perts", perts_hbm.at[0], perts),
+            ("coefs", coefs_hbm, coefs),
+            ("static", static_hbm, static),
+            ("scale", scale_hbm, scale),
+            ("weight", weight_hbm, weight),
+            ("innov", innov_hbm, innov),
+        )
+    ):
+        loads[name] = pltpu.make_async_copy(source, target, in_sem.at[place])
+        loads[name].start()
+
+    barrier = pltpu.get_barrier_semaphore()
+    for d in range(1, n):
+        pl.semaphore_signal(
+            barrier, inc=1, device_id={"tile": lax.rem(me + d, n)}, device_id_type=MESH
+        )
+
+    loads["control"].wait()
+    loads["lat"].wait()
+    smoothed = jnp.dot(
+        lat[...], control[...].astype(jnp.bfloat16), preferred_element_type=jnp.float32
+    ).astype(jnp.bfloat16)
+    loads["lon"].wait()
+    member = lax.dot_general(
+        smoothed, lon[...], (((1,), (1,)), ((), ())), preferred_element_type=jnp.float32
+    )
+    loads["perts"].wait()
+    field[0:SIDE, :] = jnp.zeros((SIDE, cols), jnp.float32)
+    field[SIDE + nlat : 2 * SIDE + nlat, :] = jnp.zeros((SIDE, cols), jnp.float32)
+    field[SIDE : SIDE + nlat, :] = perts[...].astype(jnp.float32) * member
+
+    pl.semaphore_wait(barrier, n - 1)
+
+    def window(tile):
+        return pl.ds(pl.multiple_of(tile * rows, 8), win)
+
+    member_copies = []
+    for d in range(1, n):
+        peer = lax.rem(me + d, n)
+        copy = pltpu.make_async_remote_copy(
+            src_ref=field.at[window(peer)],
+            dst_ref=received.at[me],
+            send_sem=member_send_sem.at[d],
+            recv_sem=member_recv_sem.at[d],
+            device_id={"tile": peer},
+            device_id_type=MESH,
+        )
+        copy.start()
+        member_copies.append(copy)
+    received[me] = field[window(me), :]
+
+    loads["coefs"].wait()
+    loads["static"].wait()
+    loads["scale"].wait()
+    for level in range(levels):
+        values = [coefs[k, level] for k in range(4)] + [scale[level] * static[level]]
+        for k, value in enumerate(values):
+            at = (k * levels + level) * SIDE
+            early_send[0, at : at + SIDE, :] = value[rows - SIDE : rows]
+            early_send[1, at : at + SIDE, :] = value[0:SIDE]
+            if k < 4:
+                coef_win[k, level, main, :] = value
+            else:
+                total_win[level, main, :] = value
+
+    def exchange(send, recv, send_sem, recv_sem, action):
+        def one(side, target):
+            return pltpu.make_async_remote_copy(
+                src_ref=send.at[side],
+                dst_ref=recv.at[side],
+                send_sem=send_sem.at[side],
+                recv_sem=recv_sem.at[side],
+                device_id={"tile": target},
+                device_id_type=MESH,
+            )
+
+        @pl.when(me < n - 1)
+        def _():
+            action(0, 1, functools.partial(one, target=me + 1))
+
+        @pl.when(me > 0)
+        def _():
+            action(1, 0, functools.partial(one, target=me - 1))
+
+    early = (early_send, early_recv, early_send_sem, early_recv_sem)
+    late = (late_send, late_recv, late_send_sem, late_recv_sem)
+    exchange(*early, lambda out, back, one: one(out).start())
+
+    lat_t[...] = lat[...].astype(jnp.float32).T.astype(jnp.bfloat16)
+    loads["weight"].wait()
+    loads["innov"].wait()
+    edge = jnp.zeros((SIDE, cols), jnp.float32)
+    for k in range(STEPS):
+        for level in range(levels):
+            for target, source in ((weight_win, weight), (innov_win, innov)):
+                target[k, level, 0:SIDE, :] = edge
+                target[k, level, main, :] = source[k, level]
+                target[k, level, SIDE + rows : win, :] = edge
+
+    least, largest = [], []
+    for level in range(levels):
+        low, high = jnp.int32(n - 1), jnp.int32(0)
+        for block in range(n):
+            here = level_map[block] == level
+            low = jnp.minimum(low, jnp.where(here, block, n - 1))
+            high = jnp.maximum(high, jnp.where(here, block, 0))
+        least.append(low)
+        largest.append(high)
+
+    exchange(*early, lambda out, back, one: one(back).wait_recv())
+
+    @pl.when(me == 0)
+    def _():
+        early_recv[0] = jnp.zeros(early_recv.shape[1:], jnp.float32)
+        late_recv[0] = jnp.zeros(late_recv.shape[1:], jnp.float32)
+
+    @pl.when(me == n - 1)
+    def _():
+        early_recv[1] = jnp.zeros(early_recv.shape[1:], jnp.float32)
+        late_recv[1] = jnp.zeros(late_recv.shape[1:], jnp.float32)
+
+    for level in range(levels):
+        for k in range(5):
+            at = (k * levels + level) * SIDE
+            target = coef_win.at[k, level] if k < 4 else total_win.at[level]
+            target[0:SIDE, :] = early_recv[0, at : at + SIDE, :]
+            target[SIDE + rows : win, :] = early_recv[1, at : at + SIDE, :]
+        keep_win[level] = 1.0 - (
+            coef_win[0, level] + coef_win[1, level] + coef_win[2, level] + coef_win[3, level]
+        )
+
+    for copy in member_copies:
+        copy.wait_recv()
+
+    for level in range(levels):
+        state = total_win[level] + (received[least[level]] + received[largest[level]])
+        c = [coef_win[k, level] for k in range(4)]
+        for k in range(STEPS):
+            state = (
+                state
+                + c[0] * (pltpu.roll(state, win - 1, 0) - state)
+                + c[1] * (pltpu.roll(state, 1, 0) - state)
+                + c[2] * (pltpu.roll(state, cols - 1, 1) - state)
+                + c[3] * (pltpu.roll(state, 1, 1) - state)
+            )
+            weighted[k, level] = weight_win[k, level] * (state - innov_win[k, level])
+        at = level * 8
+        for k in range(STEPS):
+            first = k * (k + 1) // 2
+            late_send[0, at + first : at + first + k + 1, :] = weighted[
+                k, level, SIDE + rows - k - 1 : SIDE + rows, :
+            ]
+            late_send[1, at + first : at + first + k + 1, :] = weighted[
+                k, level, SIDE : SIDE + k + 1, :
+            ]
+    exchange(*late, lambda out, back, one: one(out).start())
+    exchange(*late, lambda out, back, one: one(back).wait_recv())
+    for level in range(levels):
+        at = level * 8
+        for k in range(STEPS):
+            first = k * (k + 1) // 2
+            weighted[k, level, SIDE - k - 1 : SIDE, :] = late_recv[
+                0, at + first : at + first + k + 1, :
+            ]
+            weighted[k, level, SIDE + rows : SIDE + rows + k + 1, :] = late_recv[
+                1, at + first : at + first + k + 1, :
+            ]
+    for level in range(levels):
+        adjoint = weighted[STEPS - 1, level]
+        c = [coef_win[k, level] for k in range(4)]
+        for k in range(STEPS - 2, -2, -1):
+            adjoint = (
+                keep_win[level] * adjoint
+                + pltpu.roll(c[0] * adjoint, 1, 0)
+                + pltpu.roll(c[1] * adjoint, win - 1, 0)
+                + pltpu.roll(c[2] * adjoint, 1, 1)
+                + pltpu.roll(c[3] * adjoint, cols - 1, 1)
+            )
+            if k >= 0:
+                adjoint = adjoint + weighted[k, level]
+        grad[level] = adjoint[SIDE : SIDE + rows]
+
+    grad_copies = []
+    for d in range(1, n):
+        peer = lax.rem(me + d, n)
+        grad_send[d] = grad[level_map[peer]]
+        copy = pltpu.make_async_remote_copy(
+            src_ref=grad_send.at[d],
+            dst_ref=grad_field.at[me],
+            send_sem=grad_send_sem.at[d],
+            recv_sem=grad_recv_sem.at[d],
+            device_id={"tile": peer},
+            device_id_type=MESH,
+        )
+        copy.start()
+        grad_copies.append(copy)
+    grad_field[me] = grad[level_map[me]]
+
+    static_new[...] = static[...] - step_size * (static[...] + scale[...] * grad[...])
+    static_store = pltpu.make_async_copy(static_new, static_out, out_sem.at[0])
+    static_store.start()
+
+    for copy in member_copies:
+        copy.wait_send()
+    exchange(*early, lambda out, back, one: one(out).wait_send())
+    exchange(*late, lambda out, back, one: one(out).wait_send())
+    for copy in grad_copies:
+        copy.wait_recv()
+    gradient = grad_field[...].reshape(nlat, cols)
+    weighted_grad = (perts[...].astype(jnp.float32) * gradient).astype(jnp.bfloat16)
+    adjoint_lat = jnp.dot(
+        lat_t[...], weighted_grad, preferred_element_type=jnp.float32
+    ).astype(jnp.bfloat16)
+    member_grad = jnp.dot(adjoint_lat, lon[...], preferred_element_type=jnp.float32)
+    ens_new[...] = control[...] - step_size * (control[...] + member_grad)
+    ens_store = pltpu.make_async_copy(ens_new, ens_out.at[0], out_sem.at[1])
+    ens_store.start()
+    for copy in grad_copies:
+        copy.wait_send()
+    static_store.wait()
+    ens_store.wait()
+
+
+def fused(n, *args):
+    level_map, loc_lat, loc_lon, ens_perts, ens_control, static_control = args[:6]
+    nlat, cols = ens_control.shape[1:]
+    levels, rows, _ = static_control.shape
+    win = rows + 2 * SIDE
+    f32, bf16 = jnp.float32, jnp.bfloat16
+    anywhere = pl.BlockSpec(memory_space=pl.ANY)
+    dma = pltpu.SemaphoreType.DMA
+    fields = (levels, rows, cols)
+    windows = (levels, win, cols)
+    return pl.pallas_call(
+        functools.partial(kernel, n),
+        out_shape=(
+            jax.ShapeDtypeStruct(ens_control.shape, f32),
+            jax.ShapeDtypeStruct(static_control.shape, f32),
+        ),
+        in_specs=[pl.BlockSpec(memory_space=pltpu.SMEM)] + [anywhere] * 9,
+        out_specs=(anywhere, anywhere),
+        scratch_shapes=[
+            pltpu.VMEM(loc_lat.shape, bf16),
+            pltpu.VMEM(loc_lon.shape, bf16),
+            pltpu.VMEM((nlat, cols), bf16),
+            pltpu.VMEM((nlat, cols), f32),
+            pltpu.VMEM(fields, f32),
+            pltpu.VMEM(fields, f32),
+            pltpu.VMEM((4,) + fields, f32),
+            pltpu.VMEM((STEPS,) + fields, f32),
+            pltpu.VMEM((STEPS,) + fields, f32),
+            pltpu.VMEM(loc_lat.shape, bf16),
+            pltpu.VMEM((nlat + 2 * SIDE, cols), f32),
+            pltpu.VMEM((n, win, cols), f32),
+            pltpu.VMEM((4,) + windows, f32),
+            pltpu.VMEM(windows, f32),
+            pltpu.VMEM(windows, f32),
+            pltpu.VMEM((STEPS,) + windows, f32),
+            pltpu.VMEM((STEPS,) + windows, f32),
+            pltpu.VMEM((STEPS,) + windows, f32),
+            pltpu.VMEM((2, 5 * levels * SIDE, cols), f32),
+            pltpu.VMEM((2, 5 * levels * SIDE, cols), f32),
+            pltpu.VMEM((2, levels * 8, cols), f32),
+            pltpu.VMEM((2, levels * 8, cols), f32),
+            pltpu.VMEM(fields, f32),
+            pltpu.VMEM((n, rows, cols), f32),
+            pltpu.VMEM((n, rows, cols), f32),
+            pltpu.VMEM((nlat, cols), f32),
+            pltpu.VMEM(fields, f32),
+            dma((9,)),
+            dma((2,)),
+            dma((n,)),
+            dma((n,)),
+            dma((2,)),
+            dma((2,)),
+            dma((2,)),
+            dma((2,)),
+            dma((n,)),
+            dma((n,)),
+        ],
+        compiler_params=pltpu.CompilerParams(
+            collective_id=0, has_side_effects=True, vmem_limit_bytes=48 * 1024 * 1024
+        ),
+    )(*args)
+
+
+def device_program(n, *args):
+    ens_control, static_control = args[4:6]
+    levels, rows, cols = static_control.shape
+    fits = (
+        ens_control.shape[0] == 1
+        and n == 2 * levels
+        and rows % 8 == 0
+        and rows * n == ens_control.shape[1]
+        and cols % 128 == 0
+        and STEPS < SIDE
+    )
+    return fused(n, *args) if fits else local(*args)
+
+
 def solution(mesh):
     in_specs = (
         P(),
@@ -122,4 +494,5 @@
         P(None, "groups", "tile", None),
     )
     out_specs = (P(("groups", "tile"), None, None), P("groups", "tile", None))
-    return jax.shard_map(local, mesh=mesh, in_specs=in_specs, out_specs=out_specs, check_vma=False)
+    body = functools.partial(device_program, mesh.shape["tile"])
+    return jax.shard_map(body, mesh=mesh, in_specs=in_specs, out_specs=out_specs, check_vma=False)

time: 130 us -> 41.3 us (0.32)
  waiting for transfers between devices: 51.4 us -> 0 us
  starting transfers between devices: 34 us -> 0 us
  Pallas kernels: 0 us -> 29.8 us
  blocking collectives: 17.2 us -> 0 us
  between operations: 16.3 us -> 0.66 us
  local copies, waits for them, and re-layouts: 2.66 us -> 10.5 us
  matrix products: 4.64 us -> 0 us
  other arithmetic: 2.97 us -> 0 us
    all_gather x1 -> x0, waiting for transfers between devices: 41.2 us -> none  [local(): gathered = lax.all_gather(gradient, 'tile', axis=1, tiled=True)]
    ppermute x12 -> x0, starting transfers between devices: 34 us -> none  [the longest x6 26.2 us: extended(): lax.ppermute(lax.slice_in_dim(block, block.shape[dim] - width, None, axis...]
    pallas_call x0 -> x1, Pallas kernels: none -> 29.8 us  [fused(): pl.pallas_call(functools.partial(kernel, n), out_shape=(jax.ShapeDtypeStr...]
    all_to_all x1 -> x0, blocking collectives: 17.2 us -> none  [local(): lax.all_to_all(pieces, 'tile', split_axis=0, concat_axis=0, tiled=True)]
    ppermute x12 -> x0, waiting for transfers between devices: 10.1 us -> none  [the longest x6 7.93 us: extended(): lax.ppermute(lax.slice_in_dim(block, 0, width, axis=dim), axis, backward)]
    unnamed x20 -> x22, local copies, waits for them, and re-layouts: 0.9 us -> 10.5 us
    dot_general x3 -> x0, matrix products: 4.64 us -> none  [the longest x1 2.12 us: local(): jnp.einsum('bij,jk->bik', adjoint_lat, loc_lon, preferred_element_type=jn...]
  transfers between devices with their start and end apart: 13 -> 0, of which waited for: 7 -> 0; matrix products, arithmetic and copies ran while one was open for 1% -> 0% of each run, Pallas kernels for 0% -> 0%
where the time goes in v1:
time: 41.3 us; the launch traced here: 40.9 us
  Pallas kernels  29.8 us (72%)
  local copies, waits for them, and re-layouts  10.5 us (25%)
  between operations  0.66 us (2%)
    pallas_call x1, Pallas kernels, fused(): pl.pallas_call(functools.partial(kernel, n), out_shape=(jax.ShapeDtypeStr...  29.8 us
    unnamed x22, local copies, waits for them, and re-layouts  10.5 us

profile of v1, /device:TPU:0, one launch (start us, length us, event | category | flops | bytes accessed | tf_op | source)
XLA Modules:
  0.0 40.9 jit_solution(586063940669857485)
XLA Ops:
  0.6 0.0 copy-start
  0.6 1.0 %copy-done = f32[4,8,16,256]{3,2,1,0:T(8,128)S(1)} copy-done((f32[4,8,16,256]{3,2,1,0:T(8,128)S(1)}, f32[4,8,16,256]{3,2,1,0:T(8,128)}, u32[]{:S(2)}) %copy-start) | copy-done | bytes 524312
  1.7 0.0 copy-start.1
  1.7 1.0 %copy-done.1 = f32[3,8,16,256]{3,2,1,0:T(8,128)S(1)} copy-done((f32[3,8,16,256]{3,2,1,0:T(8,128)S(1)}, f32[3,8,16,256]{3,2,1,0:T(8,128)}, u32[]{:S(2)}) %copy-start.1) | copy-done | bytes 393240
  2.7 0.0 copy-start.2
  2.7 1.0 %copy-done.2 = f32[3,8,16,256]{3,2,1,0:T(8,128)S(1)} copy-done((f32[3,8,16,256]{3,2,1,0:T(8,128)S(1)}, f32[3,8,16,256]{3,2,1,0:T(8,128)}, u32[]{:S(2)}) %copy-start.2) | copy-done | bytes 393240
  3.7 0.0 copy-start.3
  3.7 0.9 %copy-done.3 = f32[1,256,256]{2,1,0:T(8,128)S(1)} copy-done((f32[1,256,256]{2,1,0:T(8,128)S(1)}, f32[1,256,256]{2,1,0:T(8,128)}, u32[]{:S(2)}) %copy-start.3) | copy-done | bytes 262168
  4.6 0.0 copy-start.4
  4.6 0.9 %copy-done.4 = bf16[256,256]{1,0:T(8,128)(2,1)S(1)} copy-done((bf16[256,256]{1,0:T(8,128)(2,1)S(1)}, bf16[256,256]{1,0:T(8,128)(2,1)}, u32[]{:S(2)}) %copy-start.4) | copy-done | bytes 131096
  5.5 0.0 copy-start.5
  5.5 0.9 %copy-done.5 = bf16[256,256]{1,0:T(8,128)(2,1)S(1)} copy-done((bf16[256,256]{1,0:T(8,128)(2,1)S(1)}, bf16[256,256]{1,0:T(8,128)(2,1)}, u32[]{:S(2)}) %copy-start.5) | copy-done | bytes 131096
  6.4 0.0 copy-start.6
  6.4 0.9 %copy-done.6 = bf16[1,256,256]{2,1,0:T(8,128)(2,1)S(1)} copy-done((bf16[1,256,256]{2,1,0:T(8,128)(2,1)S(1)}, bf16[1,256,256]{2,1,0:T(8,128)(2,1)}, u32[]{:S(2)}) %copy-start.6) | copy-done | bytes 131096
  7.3 0.0 copy-start.7
  7.3 0.9 %copy-done.7 = f32[8,16,256]{2,1,0:T(8,128)S(1)} copy-done((f32[8,16,256]{2,1,0:T(8,128)S(1)}, f32[8,16,256]{2,1,0:T(8,128)}, u32[]{:S(2)}) %copy-start.7) | copy-done | bytes 131096
  8.2 0.0 copy-start.8
  8.2 0.9 %copy-done.8 = f32[8,16,256]{2,1,0:T(8,128)S(1)} copy-done((f32[8,16,256]{2,1,0:T(8,128)S(1)}, f32[8,16,256]{2,1,0:T(8,128)}, u32[]{:S(2)}) %copy-start.8) | copy-done | bytes 131096
  9.1 0.0 copy-start.9
  9.1 0.7 %copy-done.9 = s32[16]{0:T(128)S(1)} copy-done((s32[16]{0:T(128)S(1)}, s32[16]{0:T(128)}, u32[]{:S(2)}) %copy-start.9) | copy-done | bytes 88
  9.8 29.8 %shard_map.113 = (f32[1,256,256]{2,1,0:T(8,128)S(1)}, f32[8,16,256]{2,1,0:T(8,128)S(1)}) custom-call(s32[16]{0:T(128)S(1)} %copy-done.9, bf16[256,256]{1,0:T(8,128)(2,1)S(1)} %copy-done.4, bf16[256,256]{1,0:T(8,128)(2,1)S(1)} %copy-done.5, bf16[1,256,256]{2,1,0:T(8,128)(2,1)S(1)} %copy-done.6, f32[1,256,256]{2,1,0:T(8,128)S(1)} %copy-done.3, ...), custom_call_target="tpu_custom_call" | custom-call | tf_op jit(solution)/shard_map/pallas_call | solution.py:416
  39.6 0.7 %copy.14 = f32[1,256,256]{2,1,0:T(8,128)} copy(f32[1,256,256]{2,1,0:T(8,128)S(1)} %get-tuple-element.4) | data formatting | bytes 524288
  40.3 0.7 %copy.15 = f32[8,16,256]{2,1,0:T(8,128)} copy(f32[8,16,256]{2,1,0:T(8,128)S(1)} %get-tuple-element.5) | data formatting | bytes 262144
Async XLA Ops:
  0.6 1.0 %copy-start = (f32[4,8,16,256]{3,2,1,0:T(8,128)S(1)}, f32[4,8,16,256]{3,2,1,0:T(8,128)}, u32[]{:S(2)}) copy-start(f32[4,8,16,256]{3,2,1,0:T(8,128)} %coefs_hbm.1) | copy-start | bytes 1572868
  1.7 1.0 %copy-start.1 = (f32[3,8,16,256]{3,2,1,0:T(8,128)S(1)}, f32[3,8,16,256]{3,2,1,0:T(8,128)}, u32[]{:S(2)}) copy-start(f32[3,8,16,256]{3,2,1,0:T(8,128)} %weight_hbm.1) | copy-start | bytes 1179652
  2.7 1.0 %copy-start.2 = (f32[3,8,16,256]{3,2,1,0:T(8,128)S(1)}, f32[3,8,16,256]{3,2,1,0:T(8,128)}, u32[]{:S(2)}) copy-start(f32[3,8,16,256]{3,2,1,0:T(8,128)} %innov_hbm.1) | copy-start | bytes 1179652
  3.7 0.9 %copy-start.3 = (f32[1,256,256]{2,1,0:T(8,128)S(1)}, f32[1,256,256]{2,1,0:T(8,128)}, u32[]{:S(2)}) copy-start(f32[1,256,256]{2,1,0:T(8,128)} %control_hbm.1) | copy-start | bytes 786436
  4.6 0.9 %copy-start.4 = (bf16[256,256]{1,0:T(8,128)(2,1)S(1)}, bf16[256,256]{1,0:T(8,128)(2,1)}, u32[]{:S(2)}) copy-start(bf16[256,256]{1,0:T(8,128)(2,1)} %lat_hbm.1) | copy-start | bytes 393220
  5.5 0.9 %copy-start.5 = (bf16[256,256]{1,0:T(8,128)(2,1)S(1)}, bf16[256,256]{1,0:T(8,128)(2,1)}, u32[]{:S(2)}) copy-start(bf16[256,256]{1,0:T(8,128)(2,1)} %lon_hbm.1) | copy-start | bytes 393220
  6.4 0.9 %copy-start.6 = (bf16[1,256,256]{2,1,0:T(8,128)(2,1)S(1)}, bf16[1,256,256]{2,1,0:T(8,128)(2,1)}, u32[]{:S(2)}) copy-start(bf16[1,256,256]{2,1,0:T(8,128)(2,1)} %perts_hbm.1) | copy-start | bytes 393220
  7.3 0.9 %copy-start.7 = (f32[8,16,256]{2,1,0:T(8,128)S(1)}, f32[8,16,256]{2,1,0:T(8,128)}, u32[]{:S(2)}) copy-start(f32[8,16,256]{2,1,0:T(8,128)} %static_hbm.1) | copy-start | bytes 393220
  8.2 0.9 %copy-start.8 = (f32[8,16,256]{2,1,0:T(8,128)S(1)}, f32[8,16,256]{2,1,0:T(8,128)}, u32[]{:S(2)}) copy-start(f32[8,16,256]{2,1,0:T(8,128)} %scale_hbm.1) | copy-start | bytes 393220
  9.1 0.7 %copy-start.9 = (s32[16]{0:T(128)S(1)}, s32[16]{0:T(128)}, u32[]{:S(2)}) copy-start(s32[16]{0:T(128)} %level_map.1) | copy-start | bytes 196

commit v2 on v1

--- a/solution.py
+++ b/solution.py
@@ -118,7 +118,7 @@
 
 def kernel(
     n,
-    level_map,
+    level_hbm,
     lat_hbm,
     lon_hbm,
     perts_hbm,
@@ -130,6 +130,8 @@
     innov_hbm,
     ens_out,
     static_out,
+    level_map,
+    blocks_of,
     lat,
     lon,
     perts,
@@ -174,6 +176,14 @@
     win = rows + 2 * SIDE
     main = slice(SIDE, SIDE + rows)
 
+    def each_level(body):
+        def two(pair, carry):
+            for half in range(2):
+                body(pair, half, 2 * pair + half)
+            return carry
+
+        lax.fori_loop(0, levels // 2, two, 0)
+
     loads = {}
     for place, (name, source, target) in enumerate(
         (
@@ -190,6 +200,8 @@
     ):
         loads[name] = pltpu.make_async_copy(source, target, in_sem.at[place])
         loads[name].start()
+    level_load = pltpu.make_async_copy(level_hbm, level_map, out_sem.at[2])
+    level_load.start()
 
     barrier = pltpu.get_barrier_semaphore()
     for d in range(1, n):
@@ -216,8 +228,9 @@
     def window(tile):
         return pl.ds(pl.multiple_of(tile * rows, 8), win)
 
+    order = sorted(range(1, n), key=lambda d: abs(2 * d - n))
     member_copies = []
-    for d in range(1, n):
+    for d in order:
         peer = lax.rem(me + d, n)
         copy = pltpu.make_async_remote_copy(
             src_ref=field.at[window(peer)],
@@ -234,16 +247,19 @@
     loads["coefs"].wait()
     loads["static"].wait()
     loads["scale"].wait()
-    for level in range(levels):
-        values = [coefs[k, level] for k in range(4)] + [scale[level] * static[level]]
-        for k, value in enumerate(values):
-            at = (k * levels + level) * SIDE
-            early_send[0, at : at + SIDE, :] = value[rows - SIDE : rows]
-            early_send[1, at : at + SIDE, :] = value[0:SIDE]
-            if k < 4:
-                coef_win[k, level, main, :] = value
-            else:
-                total_win[level, main, :] = value
+
+    def early_rows(pair, half, level):
+        for k in range(4):
+            early_send[0, level, 2 * k : 2 * k + 2, :] = coefs[k, level, rows - 2 : rows, :]
+            early_send[1, level, 2 * k : 2 * k + 2, :] = coefs[k, level, 0:2, :]
+            coef_win[k, level, main, :] = coefs[k, level]
+        value = scale[level] * static[level]
+        at = half * SIDE
+        early_send[0, levels + pair, at : at + SIDE, :] = value[rows - SIDE : rows]
+        early_send[1, levels + pair, at : at + SIDE, :] = value[0:SIDE]
+        total_win[level, main, :] = value
+
+    each_level(early_rows)
 
     def exchange(send, recv, send_sem, recv_sem, action):
         def one(side, target):
@@ -272,22 +288,29 @@
     loads["weight"].wait()
     loads["innov"].wait()
     edge = jnp.zeros((SIDE, cols), jnp.float32)
-    for k in range(STEPS):
-        for level in range(levels):
+
+    def widen(pair, half, level):
+        for k in range(STEPS):
             for target, source in ((weight_win, weight), (innov_win, innov)):
                 target[k, level, 0:SIDE, :] = edge
                 target[k, level, main, :] = source[k, level]
                 target[k, level, SIDE + rows : win, :] = edge
 
-    least, largest = [], []
-    for level in range(levels):
+    each_level(widen)
+
+    level_load.wait()
+
+    def find(level, carry):
         low, high = jnp.int32(n - 1), jnp.int32(0)
         for block in range(n):
             here = level_map[block] == level
             low = jnp.minimum(low, jnp.where(here, block, n - 1))
             high = jnp.maximum(high, jnp.where(here, block, 0))
-        least.append(low)
-        largest.append(high)
+        blocks_of[0, level] = low
+        blocks_of[1, level] = high
+        return carry
+
+    lax.fori_loop(0, levels, find, 0)
 
     exchange(*early, lambda out, back, one: one(back).wait_recv())
 
@@ -301,21 +324,32 @@
         early_recv[1] = jnp.zeros(early_recv.shape[1:], jnp.float32)
         late_recv[1] = jnp.zeros(late_recv.shape[1:], jnp.float32)
 
-    for level in range(levels):
-        for k in range(5):
-            at = (k * levels + level) * SIDE
-            target = coef_win.at[k, level] if k < 4 else total_win.at[level]
-            target[0:SIDE, :] = early_recv[0, at : at + SIDE, :]
-            target[SIDE + rows : win, :] = early_recv[1, at : at + SIDE, :]
+    def unpack_early(pair, half, level):
+        at = half * SIDE
+        for k in range(4):
+            coef_win[k, level, 0 : SIDE - 2, :] = jnp.full(
+                (SIDE - 2, cols), 1.0 if k == 0 else 0.0, jnp.float32
+            )
+            coef_win[k, level, SIDE - 2 : SIDE, :] = early_recv[0, level, 2 * k : 2 * k + 2, :]
+            coef_win[k, level, SIDE + rows : SIDE + rows + 2, :] = early_recv[
+                1, level, 2 * k : 2 * k + 2, :
+            ]
+            coef_win[k, level, SIDE + rows + 2 : win, :] = jnp.full(
+                (SIDE - 2, cols), 1.0 if k == 1 else 0.0, jnp.float32
+            )
+        total_win[level, 0:SIDE, :] = early_recv[0, levels + pair, at : at + SIDE, :]
+        total_win[level, SIDE + rows : win, :] = early_recv[1, levels + pair, at : at + SIDE, :]
         keep_win[level] = 1.0 - (
             coef_win[0, level] + coef_win[1, level] + coef_win[2, level] + coef_win[3, level]
         )
 
+    each_level(unpack_early)
+
     for copy in member_copies:
         copy.wait_recv()
 
-    for level in range(levels):
-        state = total_win[level] + (received[least[level]] + received[largest[level]])
+    def forward(pair, half, level):
+        state = total_win[level] + (received[blocks_of[0, level]] + received[blocks_of[1, level]])
         c = [coef_win[k, level] for k in range(4)]
         for k in range(STEPS):
             state = (
@@ -325,29 +359,33 @@
                 + c[2] * (pltpu.roll(state, cols - 1, 1) - state)
                 + c[3] * (pltpu.roll(state, 1, 1) - state)
             )
-            weighted[k, level] = weight_win[k, level] * (state - innov_win[k, level])
-        at = level * 8
-        for k in range(STEPS):
-            first = k * (k + 1) // 2
-            late_send[0, at + first : at + first + k + 1, :] = weighted[
-                k, level, SIDE + rows - k - 1 : SIDE + rows, :
-            ]
-            late_send[1, at + first : at + first + k + 1, :] = weighted[
-                k, level, SIDE : SIDE + k + 1, :
-            ]
+            value = weight_win[k, level] * (state - innov_win[k, level])
+            weighted[k, level] = value
+            at = k * (k + 1) // 2
+            low, high = SIDE, SIDE + rows
+            near = min(k + 1, 2)
+            late_send[0, level, at : at + near, :] = value[high - near : high]
+            late_send[1, level, at : at + near, :] = value[low : low + near]
+            if k == 2:
+                late_send[0, level, at + 2 : at + 3, :] = (c[0] * value)[high - 3 : high - 2]
+                late_send[1, level, at + 2 : at + 3, :] = (c[1] * value)[low + 2 : low + 3]
+
+    each_level(forward)
     exchange(*late, lambda out, back, one: one(out).start())
     exchange(*late, lambda out, back, one: one(back).wait_recv())
-    for level in range(levels):
-        at = level * 8
+
+    def backward(pair, half, level):
         for k in range(STEPS):
-            first = k * (k + 1) // 2
-            weighted[k, level, SIDE - k - 1 : SIDE, :] = late_recv[
-                0, at + first : at + first + k + 1, :
-            ]
-            weighted[k, level, SIDE + rows : SIDE + rows + k + 1, :] = late_recv[
-                1, at + first : at + first + k + 1, :
-            ]
-    for level in range(levels):
+            at = k * (k + 1) // 2
+            low, high = SIDE, SIDE + rows
+            near = min(k + 1, 2)
+            weighted[k, level, low - near : low, :] = late_recv[0, level, at : at + near, :]
+            weighted[k, level, high : high + near, :] = late_recv[1, level, at : at + near, :]
+            if k == 2:
+                weighted[k, level, low - 3 : low - 2, :] = late_recv[0, level, at + 2 : at + 3, :]
+                weighted[k, level, high + 2 : high + 3, :] = late_recv[
+                    1, level, at + 2 : at + 3, :
+                ]
         adjoint = weighted[STEPS - 1, level]
         c = [coef_win[k, level] for k in range(4)]
         for k in range(STEPS - 2, -2, -1):
@@ -362,8 +400,10 @@
                 adjoint = adjoint + weighted[k, level]
         grad[level] = adjoint[SIDE : SIDE + rows]
 
+    each_level(backward)
+
     grad_copies = []
-    for d in range(1, n):
+    for d in order:
         peer = lax.rem(me + d, n)
         grad_send[d] = grad[level_map[peer]]
         copy = pltpu.make_async_remote_copy(
@@ -419,9 +459,11 @@
             jax.ShapeDtypeStruct(ens_control.shape, f32),
             jax.ShapeDtypeStruct(static_control.shape, f32),
         ),
-        in_specs=[pl.BlockSpec(memory_space=pltpu.SMEM)] + [anywhere] * 9,
+        in_specs=[pl.BlockSpec(memory_space=pltpu.HBM)] * 10,
         out_specs=(anywhere, anywhere),
         scratch_shapes=[
+            pltpu.SMEM(level_map.shape, jnp.int32),
+            pltpu.SMEM((2, levels), jnp.int32),
             pltpu.VMEM(loc_lat.shape, bf16),
             pltpu.VMEM(loc_lon.shape, bf16),
             pltpu.VMEM((nlat, cols), bf16),
@@ -440,17 +482,17 @@
             pltpu.VMEM((STEPS,) + windows, f32),
             pltpu.VMEM((STEPS,) + windows, f32),
             pltpu.VMEM((STEPS,) + windows, f32),
-            pltpu.VMEM((2, 5 * levels * SIDE, cols), f32),
-            pltpu.VMEM((2, 5 * levels * SIDE, cols), f32),
-            pltpu.VMEM((2, levels * 8, cols), f32),
-            pltpu.VMEM((2, levels * 8, cols), f32),
+            pltpu.VMEM((2, levels + levels // 2, 8, cols), f32),
+            pltpu.VMEM((2, levels + levels // 2, 8, cols), f32),
+            pltpu.VMEM((2, levels, 8, cols), f32),
+            pltpu.VMEM((2, levels, 8, cols), f32),
             pltpu.VMEM(fields, f32),
             pltpu.VMEM((n, rows, cols), f32),
             pltpu.VMEM((n, rows, cols), f32),
             pltpu.VMEM((nlat, cols), f32),
             pltpu.VMEM(fields, f32),
             dma((9,)),
-            dma((2,)),
+            dma((3,)),
             dma((n,)),
             dma((n,)),
             dma((2,)),
@@ -475,7 +517,8 @@
         and rows % 8 == 0
         and rows * n == ens_control.shape[1]
         and cols % 128 == 0
-        and STEPS < SIDE
+        and levels % 2 == 0
+        and STEPS == 3
     )
     return fused(n, *args) if fits else local(*args)
 

time: 41.3 us -> 41.5 us (level)
  no operation moved by 1% of the time
where the time goes in v2:
time: 41.5 us; the launch traced here: 41.1 us
  Pallas kernels  29.9 us (72%)
  local copies, waits for them, and re-layouts  10.5 us (25%)
  between operations  0.66 us (2%)
    pallas_call x1, Pallas kernels, fused(): pl.pallas_call(functools.partial(kernel, n), out_shape=(jax.ShapeDtypeStr...  29.9 us
    unnamed x22, local copies, waits for them, and re-layouts  10.5 us

profile of v2, /device:TPU:0, one launch (start us, length us, event | category | flops | bytes accessed | tf_op | source)
XLA Modules:
  0.0 41.1 jit_solution(12658600812520308507)
XLA Ops:
  0.6 0.0 copy-start
  0.6 1.0 %copy-done = f32[4,8,16,256]{3,2,1,0:T(8,128)S(1)} copy-done((f32[4,8,16,256]{3,2,1,0:T(8,128)S(1)}, f32[4,8,16,256]{3,2,1,0:T(8,128)}, u32[]{:S(2)}) %copy-start) | copy-done | bytes 524312
  1.7 0.0 copy-start.1
  1.7 1.0 %copy-done.1 = f32[3,8,16,256]{3,2,1,0:T(8,128)S(1)} copy-done((f32[3,8,16,256]{3,2,1,0:T(8,128)S(1)}, f32[3,8,16,256]{3,2,1,0:T(8,128)}, u32[]{:S(2)}) %copy-start.1) | copy-done | bytes 393240
  2.7 0.0 copy-start.2
  2.7 1.0 %copy-done.2 = f32[3,8,16,256]{3,2,1,0:T(8,128)S(1)} copy-done((f32[3,8,16,256]{3,2,1,0:T(8,128)S(1)}, f32[3,8,16,256]{3,2,1,0:T(8,128)}, u32[]{:S(2)}) %copy-start.2) | copy-done | bytes 393240
  3.7 0.0 copy-start.3
  3.7 0.9 %copy-done.3 = f32[1,256,256]{2,1,0:T(8,128)S(1)} copy-done((f32[1,256,256]{2,1,0:T(8,128)S(1)}, f32[1,256,256]{2,1,0:T(8,128)}, u32[]{:S(2)}) %copy-start.3) | copy-done | bytes 262168
  4.6 0.0 copy-start.4
  4.6 0.9 %copy-done.4 = bf16[256,256]{1,0:T(8,128)(2,1)S(1)} copy-done((bf16[256,256]{1,0:T(8,128)(2,1)S(1)}, bf16[256,256]{1,0:T(8,128)(2,1)}, u32[]{:S(2)}) %copy-start.4) | copy-done | bytes 131096
  5.5 0.0 copy-start.5
  5.5 0.9 %copy-done.5 = bf16[256,256]{1,0:T(8,128)(2,1)S(1)} copy-done((bf16[256,256]{1,0:T(8,128)(2,1)S(1)}, bf16[256,256]{1,0:T(8,128)(2,1)}, u32[]{:S(2)}) %copy-start.5) | copy-done | bytes 131096
  6.4 0.0 copy-start.6
  6.4 0.9 %copy-done.6 = bf16[1,256,256]{2,1,0:T(8,128)(2,1)S(1)} copy-done((bf16[1,256,256]{2,1,0:T(8,128)(2,1)S(1)}, bf16[1,256,256]{2,1,0:T(8,128)(2,1)}, u32[]{:S(2)}) %copy-start.6) | copy-done | bytes 131096
  7.3 0.0 copy-start.7
  7.3 0.9 %copy-done.7 = f32[8,16,256]{2,1,0:T(8,128)S(1)} copy-done((f32[8,16,256]{2,1,0:T(8,128)S(1)}, f32[8,16,256]{2,1,0:T(8,128)}, u32[]{:S(2)}) %copy-start.7) | copy-done | bytes 131096
  8.2 0.0 copy-start.8
  8.2 0.9 %copy-done.8 = f32[8,16,256]{2,1,0:T(8,128)S(1)} copy-done((f32[8,16,256]{2,1,0:T(8,128)S(1)}, f32[8,16,256]{2,1,0:T(8,128)}, u32[]{:S(2)}) %copy-start.8) | copy-done | bytes 131096
  9.1 0.0 copy-start.9
  9.1 0.7 %copy-done.9 = s32[16]{0:T(128)S(1)} copy-done((s32[16]{0:T(128)S(1)}, s32[16]{0:T(128)}, u32[]{:S(2)}) %copy-start.9) | copy-done | bytes 88
  9.8 29.9 %shard_map.113 = (f32[1,256,256]{2,1,0:T(8,128)S(1)}, f32[8,16,256]{2,1,0:T(8,128)S(1)}) custom-call(s32[16]{0:T(128)S(1)} %copy-done.9, bf16[256,256]{1,0:T(8,128)(2,1)S(1)} %copy-done.4, bf16[256,256]{1,0:T(8,128)(2,1)S(1)} %copy-done.5, bf16[1,256,256]{2,1,0:T(8,128)(2,1)S(1)} %copy-done.6, f32[1,256,256]{2,1,0:T(8,128)S(1)} %copy-done.3, ...), custom_call_target="tpu_custom_call" | custom-call | tf_op jit(solution)/shard_map/pallas_call | solution.py:456
  39.7 0.7 %copy.14 = f32[1,256,256]{2,1,0:T(8,128)} copy(f32[1,256,256]{2,1,0:T(8,128)S(1)} %get-tuple-element.4) | data formatting | bytes 524288
  40.4 0.7 %copy.15 = f32[8,16,256]{2,1,0:T(8,128)} copy(f32[8,16,256]{2,1,0:T(8,128)S(1)} %get-tuple-element.5) | data formatting | bytes 262144
Async XLA Ops:
  0.6 1.0 %copy-start = (f32[4,8,16,256]{3,2,1,0:T(8,128)S(1)}, f32[4,8,16,256]{3,2,1,0:T(8,128)}, u32[]{:S(2)}) copy-start(f32[4,8,16,256]{3,2,1,0:T(8,128)} %coefs_hbm.1) | copy-start | bytes 1572868
  1.7 1.0 %copy-start.1 = (f32[3,8,16,256]{3,2,1,0:T(8,128)S(1)}, f32[3,8,16,256]{3,2,1,0:T(8,128)}, u32[]{:S(2)}) copy-start(f32[3,8,16,256]{3,2,1,0:T(8,128)} %weight_hbm.1) | copy-start | bytes 1179652
  2.7 1.0 %copy-start.2 = (f32[3,8,16,256]{3,2,1,0:T(8,128)S(1)}, f32[3,8,16,256]{3,2,1,0:T(8,128)}, u32[]{:S(2)}) copy-start(f32[3,8,16,256]{3,2,1,0:T(8,128)} %innov_hbm.1) | copy-start | bytes 1179652
  3.7 0.9 %copy-start.3 = (f32[1,256,256]{2,1,0:T(8,128)S(1)}, f32[1,256,256]{2,1,0:T(8,128)}, u32[]{:S(2)}) copy-start(f32[1,256,256]{2,1,0:T(8,128)} %control_hbm.1) | copy-start | bytes 786436
  4.6 0.9 %copy-start.4 = (bf16[256,256]{1,0:T(8,128)(2,1)S(1)}, bf16[256,256]{1,0:T(8,128)(2,1)}, u32[]{:S(2)}) copy-start(bf16[256,256]{1,0:T(8,128)(2,1)} %lat_hbm.1) | copy-start | bytes 393220
  5.5 0.9 %copy-start.5 = (bf16[256,256]{1,0:T(8,128)(2,1)S(1)}, bf16[256,256]{1,0:T(8,128)(2,1)}, u32[]{:S(2)}) copy-start(bf16[256,256]{1,0:T(8,128)(2,1)} %lon_hbm.1) | copy-start | bytes 393220
  6.4 0.9 %copy-start.6 = (bf16[1,256,256]{2,1,0:T(8,128)(2,1)S(1)}, bf16[1,256,256]{2,1,0:T(8,128)(2,1)}, u32[]{:S(2)}) copy-start(bf16[1,256,256]{2,1,0:T(8,128)(2,1)} %perts_hbm.1) | copy-start | bytes 393220
  7.3 0.9 %copy-start.7 = (f32[8,16,256]{2,1,0:T(8,128)S(1)}, f32[8,16,256]{2,1,0:T(8,128)}, u32[]{:S(2)}) copy-start(f32[8,16,256]{2,1,0:T(8,128)} %static_hbm.1) | copy-start | bytes 393220
  8.2 0.9 %copy-start.8 = (f32[8,16,256]{2,1,0:T(8,128)S(1)}, f32[8,16,256]{2,1,0:T(8,128)}, u32[]{:S(2)}) copy-start(f32[8,16,256]{2,1,0:T(8,128)} %scale_hbm.1) | copy-start | bytes 393220
  9.1 0.7 %copy-start.9 = (s32[16]{0:T(128)S(1)}, s32[16]{0:T(128)}, u32[]{:S(2)}) copy-start(s32[16]{0:T(128)} %level_hbm.1) | copy-start | bytes 196

commit v3 on v2

--- a/solution.py
+++ b/solution.py
@@ -176,10 +176,14 @@
     win = rows + 2 * SIDE
     main = slice(SIDE, SIDE + rows)
 
-    def each_level(body):
+    def each_level(body, before=None, after=None):
         def two(pair, carry):
+            if before is not None:
+                before(pair)
             for half in range(2):
                 body(pair, half, 2 * pair + half)
+            if after is not None:
+                after(pair)
             return carry
 
         lax.fori_loop(0, levels // 2, two, 0)
@@ -261,13 +265,14 @@
 
     each_level(early_rows)
 
-    def exchange(send, recv, send_sem, recv_sem, action):
+    def exchange(send, recv, send_sem, recv_sem, action, chunk=0, width=None):
         def one(side, target):
+            part = (side,) if width is None else (side, pl.ds(chunk * width, width))
             return pltpu.make_async_remote_copy(
-                src_ref=send.at[side],
-                dst_ref=recv.at[side],
-                send_sem=send_sem.at[side],
-                recv_sem=recv_sem.at[side],
+                src_ref=send.at[part],
+                dst_ref=recv.at[part],
+                send_sem=send_sem.at[side, chunk],
+                recv_sem=recv_sem.at[side, chunk],
                 device_id={"tile": target},
                 device_id_type=MESH,
             )
@@ -280,9 +285,18 @@
         def _():
             action(1, 0, functools.partial(one, target=me - 1))
 
+    def start(out, back, one):
+        one(out).start()
+
+    def wait_recv(out, back, one):
+        one(back).wait_recv()
+
+    def wait_send(out, back, one):
+        one(out).wait_send()
+
     early = (early_send, early_recv, early_send_sem, early_recv_sem)
     late = (late_send, late_recv, late_send_sem, late_recv_sem)
-    exchange(*early, lambda out, back, one: one(out).start())
+    exchange(*early, start)
 
     lat_t[...] = lat[...].astype(jnp.float32).T.astype(jnp.bfloat16)
     loads["weight"].wait()
@@ -312,7 +326,7 @@
 
     lax.fori_loop(0, levels, find, 0)
 
-    exchange(*early, lambda out, back, one: one(back).wait_recv())
+    exchange(*early, wait_recv)
 
     @pl.when(me == 0)
     def _():
@@ -370,9 +384,7 @@
                 late_send[0, level, at + 2 : at + 3, :] = (c[0] * value)[high - 3 : high - 2]
                 late_send[1, level, at + 2 : at + 3, :] = (c[1] * value)[low + 2 : low + 3]
 
-    each_level(forward)
-    exchange(*late, lambda out, back, one: one(out).start())
-    exchange(*late, lambda out, back, one: one(back).wait_recv())
+    each_level(forward, after=lambda pair: exchange(*late, start, pair, 2))
 
     def backward(pair, half, level):
         for k in range(STEPS):
@@ -400,7 +412,7 @@
                 adjoint = adjoint + weighted[k, level]
         grad[level] = adjoint[SIDE : SIDE + rows]
 
-    each_level(backward)
+    each_level(backward, before=lambda pair: exchange(*late, wait_recv, pair, 2))
 
     grad_copies = []
     for d in order:
@@ -424,8 +436,8 @@
 
     for copy in member_copies:
         copy.wait_send()
-    exchange(*early, lambda out, back, one: one(out).wait_send())
-    exchange(*late, lambda out, back, one: one(out).wait_send())
+    exchange(*early, wait_send)
+    each_level(lambda *_: None, before=lambda pair: exchange(*late, wait_send, pair, 2))
     for copy in grad_copies:
         copy.wait_recv()
     gradient = grad_field[...].reshape(nlat, cols)
@@ -495,15 +507,15 @@
             dma((3,)),
             dma((n,)),
             dma((n,)),
-            dma((2,)),
-            dma((2,)),
-            dma((2,)),
-            dma((2,)),
+            dma((2, 1)),
+            dma((2, 1)),
+            dma((2, levels // 2)),
+            dma((2, levels // 2)),
             dma((n,)),
             dma((n,)),
         ],
         compiler_params=pltpu.CompilerParams(
-            collective_id=0, has_side_effects=True, vmem_limit_bytes=48 * 1024 * 1024
+            collective_id=0, has_side_effects=True
         ),
     )(*args)
 

time: 41.5 us -> 31.7 us (0.76)
  local copies, waits for them, and re-layouts: 10.5 us -> 2.36 us
  Pallas kernels: 29.9 us -> 28.5 us
    unnamed x22 -> x4, local copies, waits for them, and re-layouts: 10.5 us -> 2.36 us
    pallas_call x1, Pallas kernels: 29.9 us -> 28.5 us  [fused(): pl.pallas_call(functools.partial(kernel, n), out_shape=(jax.ShapeDtypeStr...]
where the time goes in v3:
time: 31.7 us; the launch traced here: 31.5 us
  Pallas kernels  28.5 us (90%)
  local copies, waits for them, and re-layouts  2.36 us (7%)
  between operations  0.65 us (2%)
    pallas_call x1, Pallas kernels, fused(): pl.pallas_call(functools.partial(kernel, n), out_shape=(jax.ShapeDtypeStr...  28.5 us
    unnamed x4, local copies, waits for them, and re-layouts  2.36 us

profile of v3, /device:TPU:0, one launch (start us, length us, event | category | flops | bytes accessed | tf_op | source)
XLA Modules:
  0.0 31.5 jit_solution(3335652657080134052)
XLA Ops:
  0.6 28.5 %shard_map.113 = (f32[1,256,256]{2,1,0:T(8,128)}, f32[8,16,256]{2,1,0:T(8,128)}) custom-call(s32[16]{0:T(128)} %level_hbm.1, bf16[256,256]{1,0:T(8,128)(2,1)} %lat_hbm.1, bf16[256,256]{1,0:T(8,128)(2,1)} %lon_hbm.1, bf16[1,256,256]{2,1,0:T(8,128)(2,1)} %perts_hbm.1, f32[1,256,256]{2,1,0:T(8,128)} %control_hbm.1, f32[8,16,256]{2,1,0:T(8,128)} %static_hbm.1, ...), custom_call_target="tpu_custom_call" | custom-call | tf_op jit(solution)/shard_map/pallas_call | solution.py:468
  29.2 0.0 copy-start
  29.2 1.7 %copy.14 = f32[1,256,256]{2,1,0:T(8,128)} copy(f32[1,256,256]{2,1,0:T(8,128)} %get-tuple-element.4) | data formatting | bytes 524288
  30.9 0.0 copy-done
  30.9 0.7 %copy.15 = f32[8,16,256]{2,1,0:T(8,128)} copy(f32[8,16,256]{2,1,0:T(8,128)S(1)} %copy-done) | data formatting | bytes 262144
Async XLA Ops:
  29.2 1.7 %copy-start = (f32[8,16,256]{2,1,0:T(8,128)S(1)}, f32[8,16,256]{2,1,0:T(8,128)}, u32[]{:S(2)}) copy-start(f32[8,16,256]{2,1,0:T(8,128)} %get-tuple-element.5) | copy-start | bytes 393220

commit v4 on v3

--- a/solution.py
+++ b/solution.py
@@ -128,8 +128,9 @@
     coefs_hbm,
     weight_hbm,
     innov_hbm,
-    ens_out,
+    grad_field,
     static_out,
+    lat_out,
     level_map,
     blocks_of,
     lat,
@@ -152,12 +153,12 @@
     weighted,
     early_send,
     early_recv,
+    mid_send,
+    mid_recv,
     late_send,
     late_recv,
     grad,
     grad_send,
-    grad_field,
-    ens_new,
     static_new,
     in_sem,
     out_sem,
@@ -165,6 +166,8 @@
     member_recv_sem,
     early_send_sem,
     early_recv_sem,
+    mid_send_sem,
+    mid_recv_sem,
     late_send_sem,
     late_recv_sem,
     grad_send_sem,
@@ -223,21 +226,19 @@
         smoothed, lon[...], (((1,), (1,)), ((), ())), preferred_element_type=jnp.float32
     )
     loads["perts"].wait()
-    field[0:SIDE, :] = jnp.zeros((SIDE, cols), jnp.float32)
-    field[SIDE + nlat : 2 * SIDE + nlat, :] = jnp.zeros((SIDE, cols), jnp.float32)
-    field[SIDE : SIDE + nlat, :] = perts[...].astype(jnp.float32) * member
+    field[...] = perts[...].astype(jnp.float32) * member
 
     pl.semaphore_wait(barrier, n - 1)
 
-    def window(tile):
-        return pl.ds(pl.multiple_of(tile * rows, 8), win)
+    def piece(tile):
+        return pl.ds(pl.multiple_of(tile * rows, 8), rows)
 
     order = sorted(range(1, n), key=lambda d: abs(2 * d - n))
     member_copies = []
     for d in order:
         peer = lax.rem(me + d, n)
         copy = pltpu.make_async_remote_copy(
-            src_ref=field.at[window(peer)],
+            src_ref=field.at[piece(peer)],
             dst_ref=received.at[me],
             send_sem=member_send_sem.at[d],
             recv_sem=member_recv_sem.at[d],
@@ -246,7 +247,7 @@
         )
         copy.start()
         member_copies.append(copy)
-    received[me] = field[window(me), :]
+    received[me] = field[piece(me), :]
 
     loads["coefs"].wait()
     loads["static"].wait()
@@ -257,11 +258,6 @@
             early_send[0, level, 2 * k : 2 * k + 2, :] = coefs[k, level, rows - 2 : rows, :]
             early_send[1, level, 2 * k : 2 * k + 2, :] = coefs[k, level, 0:2, :]
             coef_win[k, level, main, :] = coefs[k, level]
-        value = scale[level] * static[level]
-        at = half * SIDE
-        early_send[0, levels + pair, at : at + SIDE, :] = value[rows - SIDE : rows]
-        early_send[1, levels + pair, at : at + SIDE, :] = value[0:SIDE]
-        total_win[level, main, :] = value
 
     each_level(early_rows)
 
@@ -295,10 +291,13 @@
         one(out).wait_send()
 
     early = (early_send, early_recv, early_send_sem, early_recv_sem)
+    mid = (mid_send, mid_recv, mid_send_sem, mid_recv_sem)
     late = (late_send, late_recv, late_send_sem, late_recv_sem)
     exchange(*early, start)
 
     lat_t[...] = lat[...].astype(jnp.float32).T.astype(jnp.bfloat16)
+    lat_store = pltpu.make_async_copy(lat_t, lat_out, out_sem.at[1])
+    lat_store.start()
     loads["weight"].wait()
     loads["innov"].wait()
     edge = jnp.zeros((SIDE, cols), jnp.float32)
@@ -331,15 +330,16 @@
     @pl.when(me == 0)
     def _():
         early_recv[0] = jnp.zeros(early_recv.shape[1:], jnp.float32)
+        mid_recv[0] = jnp.zeros(mid_recv.shape[1:], jnp.float32)
         late_recv[0] = jnp.zeros(late_recv.shape[1:], jnp.float32)
 
     @pl.when(me == n - 1)
     def _():
         early_recv[1] = jnp.zeros(early_recv.shape[1:], jnp.float32)
+        mid_recv[1] = jnp.zeros(mid_recv.shape[1:], jnp.float32)
         late_recv[1] = jnp.zeros(late_recv.shape[1:], jnp.float32)
 
     def unpack_early(pair, half, level):
-        at = half * SIDE
         for k in range(4):
             coef_win[k, level, 0 : SIDE - 2, :] = jnp.full(
                 (SIDE - 2, cols), 1.0 if k == 0 else 0.0, jnp.float32
@@ -351,8 +351,6 @@
             coef_win[k, level, SIDE + rows + 2 : win, :] = jnp.full(
                 (SIDE - 2, cols), 1.0 if k == 1 else 0.0, jnp.float32
             )
-        total_win[level, 0:SIDE, :] = early_recv[0, levels + pair, at : at + SIDE, :]
-        total_win[level, SIDE + rows : win, :] = early_recv[1, levels + pair, at : at + SIDE, :]
         keep_win[level] = 1.0 - (
             coef_win[0, level] + coef_win[1, level] + coef_win[2, level] + coef_win[3, level]
         )
@@ -362,8 +360,22 @@
     for copy in member_copies:
         copy.wait_recv()
 
+    def add_up(pair, half, level):
+        total = scale[level] * static[level] + (
+            received[blocks_of[0, level]] + received[blocks_of[1, level]]
+        )
+        at = half * SIDE
+        mid_send[0, pair, at : at + SIDE, :] = total[rows - SIDE : rows]
+        mid_send[1, pair, at : at + SIDE, :] = total[0:SIDE]
+        total_win[level, main, :] = total
+
+    each_level(add_up, after=lambda pair: exchange(*mid, start, pair, 1))
+
     def forward(pair, half, level):
-        state = total_win[level] + (received[blocks_of[0, level]] + received[blocks_of[1, level]])
+        at = half * SIDE
+        total_win[level, 0:SIDE, :] = mid_recv[0, pair, at : at + SIDE, :]
+        total_win[level, SIDE + rows : win, :] = mid_recv[1, pair, at : at + SIDE, :]
+        state = total_win[level]
         c = [coef_win[k, level] for k in range(4)]
         for k in range(STEPS):
             state = (
@@ -384,7 +396,11 @@
                 late_send[0, level, at + 2 : at + 3, :] = (c[0] * value)[high - 3 : high - 2]
                 late_send[1, level, at + 2 : at + 3, :] = (c[1] * value)[low + 2 : low + 3]
 
-    each_level(forward, after=lambda pair: exchange(*late, start, pair, 2))
+    each_level(
+        forward,
+        before=lambda pair: exchange(*mid, wait_recv, pair, 1),
+        after=lambda pair: exchange(*late, start, pair, 2),
+    )
 
     def backward(pair, half, level):
         for k in range(STEPS):
@@ -428,7 +444,9 @@
         )
         copy.start()
         grad_copies.append(copy)
-    grad_field[me] = grad[level_map[me]]
+    grad_send[0] = grad[level_map[me]]
+    own_store = pltpu.make_async_copy(grad_send.at[0], grad_field.at[me], out_sem.at[3])
+    own_store.start()
 
     static_new[...] = static[...] - step_size * (static[...] + scale[...] * grad[...])
     static_store = pltpu.make_async_copy(static_new, static_out, out_sem.at[0])
@@ -437,22 +455,73 @@
     for copy in member_copies:
         copy.wait_send()
     exchange(*early, wait_send)
-    each_level(lambda *_: None, before=lambda pair: exchange(*late, wait_send, pair, 2))
+
+    def sent(pair):
+        exchange(*mid, wait_send, pair, 1)
+        exchange(*late, wait_send, pair, 2)
+
+    each_level(lambda *_: None, before=sent)
     for copy in grad_copies:
         copy.wait_recv()
-    gradient = grad_field[...].reshape(nlat, cols)
-    weighted_grad = (perts[...].astype(jnp.float32) * gradient).astype(jnp.bfloat16)
-    adjoint_lat = jnp.dot(
-        lat_t[...], weighted_grad, preferred_element_type=jnp.float32
-    ).astype(jnp.bfloat16)
-    member_grad = jnp.dot(adjoint_lat, lon[...], preferred_element_type=jnp.float32)
-    ens_new[...] = control[...] - step_size * (control[...] + member_grad)
-    ens_store = pltpu.make_async_copy(ens_new, ens_out.at[0], out_sem.at[1])
-    ens_store.start()
     for copy in grad_copies:
         copy.wait_send()
+    lat_store.wait()
+    own_store.wait()
     static_store.wait()
-    ens_store.wait()
+
+
+def finish_kernel(
+    grad_hbm,
+    lat_hbm,
+    lon_hbm,
+    perts_hbm,
+    control_hbm,
+    static_hbm,
+    ens_out,
+    static_out,
+    gradient,
+    lat_t,
+    lon,
+    perts,
+    control,
+    ens_new,
+    in_sem,
+    out_sem,
+):
+    loads = []
+    for place, (source, target) in enumerate(
+        (
+            (grad_hbm, gradient),
+            (perts_hbm.at[0], perts),
+            (lat_hbm, lat_t),
+            (lon_hbm, lon),
+            (control_hbm.at[0], control),
+        )
+    ):
+        loads.append(pltpu.make_async_copy(source, target, in_sem.at[place]))
+        loads[-1].start()
+    static_store = pltpu.make_async_copy(static_hbm, static_out, out_sem.at[2])
+    static_store.start()
+    for load in loads:
+        load.wait()
+    nlat, cols = control.shape
+    grad_field = gradient[...].reshape(nlat, cols)
+    weighted_grad = (perts[...].astype(jnp.float32) * grad_field).astype(jnp.bfloat16)
+    stores = []
+    for part in range(2):
+        here = slice(part * nlat // 2, (part + 1) * nlat // 2)
+        adjoint_lat = jnp.dot(
+            lat_t[here, :], weighted_grad, preferred_element_type=jnp.float32
+        ).astype(jnp.bfloat16)
+        member_grad = jnp.dot(adjoint_lat, lon[...], preferred_element_type=jnp.float32)
+        ens_new[here, :] = control[here, :] - step_size * (control[here, :] + member_grad)
+        stores.append(
+            pltpu.make_async_copy(ens_new.at[here], ens_out.at[0, here], out_sem.at[part])
+        )
+        stores[-1].start()
+    for store in stores:
+        store.wait()
+    static_store.wait()
 
 
 def fused(n, *args):
@@ -465,14 +534,15 @@
     dma = pltpu.SemaphoreType.DMA
     fields = (levels, rows, cols)
     windows = (levels, win, cols)
-    return pl.pallas_call(
+    grad_field, static_new, lat_t = pl.pallas_call(
         functools.partial(kernel, n),
         out_shape=(
-            jax.ShapeDtypeStruct(ens_control.shape, f32),
+            jax.ShapeDtypeStruct((n, rows, cols), f32),
             jax.ShapeDtypeStruct(static_control.shape, f32),
+            jax.ShapeDtypeStruct(loc_lat.shape, bf16),
         ),
         in_specs=[pl.BlockSpec(memory_space=pltpu.HBM)] * 10,
-        out_specs=(anywhere, anywhere),
+        out_specs=(anywhere, anywhere, anywhere),
         scratch_shapes=[
             pltpu.SMEM(level_map.shape, jnp.int32),
             pltpu.SMEM((2, levels), jnp.int32),
@@ -486,29 +556,31 @@
             pltpu.VMEM((STEPS,) + fields, f32),
             pltpu.VMEM((STEPS,) + fields, f32),
             pltpu.VMEM(loc_lat.shape, bf16),
-            pltpu.VMEM((nlat + 2 * SIDE, cols), f32),
-            pltpu.VMEM((n, win, cols), f32),
+            pltpu.VMEM((nlat, cols), f32),
+            pltpu.VMEM((n, rows, cols), f32),
             pltpu.VMEM((4,) + windows, f32),
             pltpu.VMEM(windows, f32),
             pltpu.VMEM(windows, f32),
             pltpu.VMEM((STEPS,) + windows, f32),
             pltpu.VMEM((STEPS,) + windows, f32),
             pltpu.VMEM((STEPS,) + windows, f32),
-            pltpu.VMEM((2, levels + levels // 2, 8, cols), f32),
-            pltpu.VMEM((2, levels + levels // 2, 8, cols), f32),
+            pltpu.VMEM((2, levels, 8, cols), f32),
+            pltpu.VMEM((2, levels, 8, cols), f32),
+            pltpu.VMEM((2, levels // 2, 8, cols), f32),
+            pltpu.VMEM((2, levels // 2, 8, cols), f32),
             pltpu.VMEM((2, levels, 8, cols), f32),
             pltpu.VMEM((2, levels, 8, cols), f32),
             pltpu.VMEM(fields, f32),
             pltpu.VMEM((n, rows, cols), f32),
-            pltpu.VMEM((n, rows, cols), f32),
-            pltpu.VMEM((nlat, cols), f32),
             pltpu.VMEM(fields, f32),
             dma((9,)),
-            dma((3,)),
+            dma((4,)),
             dma((n,)),
             dma((n,)),
             dma((2, 1)),
             dma((2, 1)),
+            dma((2, levels // 2)),
+            dma((2, levels // 2)),
             dma((2, levels // 2)),
             dma((2, levels // 2)),
             dma((n,)),
@@ -518,6 +590,25 @@
             collective_id=0, has_side_effects=True
         ),
     )(*args)
+    return pl.pallas_call(
+        finish_kernel,
+        out_shape=(
+            jax.ShapeDtypeStruct(ens_control.shape, f32),
+            jax.ShapeDtypeStruct(static_control.shape, f32),
+        ),
+        in_specs=[anywhere] * 6,
+        out_specs=(anywhere, anywhere),
+        scratch_shapes=[
+            pltpu.VMEM((n, rows, cols), f32),
+            pltpu.VMEM(loc_lat.shape, bf16),
+            pltpu.VMEM(loc_lon.shape, bf16),
+            pltpu.VMEM((nlat, cols), bf16),
+            pltpu.VMEM((nlat, cols), f32),
+            pltpu.VMEM((nlat, cols), f32),
+            dma((5,)),
+            dma((3,)),
+        ],
+    )(grad_field, lat_t, loc_lon, ens_perts, ens_control, static_new)
 
 
 def device_program(n, *args):

time: 31.7 us -> 33.2 us (1.047)
  Pallas kernels: 28.5 us -> 32.4 us
  local copies, waits for them, and re-layouts: 2.36 us -> 0 us
    pallas_call x0 -> x1, Pallas kernels: none -> 5.15 us  [fused(): pl.pallas_call(finish_kernel, out_shape=(jax.ShapeDtypeStruct(ens_control...]
    unnamed x4 -> x0, local copies, waits for them, and re-layouts: 2.36 us -> none
    pallas_call x1, Pallas kernels: 28.5 us -> 27.3 us  [fused(): pl.pallas_call(functools.partial(kernel, n), out_shape=(jax.ShapeDtypeStr...]
where the time goes in v4:
time: 33.2 us; the launch traced here: 33.1 us
  Pallas kernels  32.4 us (98%)
  between operations  0.64 us (2%)
    pallas_call x1, Pallas kernels, fused(): pl.pallas_call(functools.partial(kernel, n), out_shape=(jax.ShapeDtypeStr...  27.3 us
    pallas_call x1, Pallas kernels, fused(): pl.pallas_call(finish_kernel, out_shape=(jax.ShapeDtypeStruct(ens_control...  5.15 us

profile of v4, /device:TPU:0, one launch (start us, length us, event | category | flops | bytes accessed | tf_op | source)
XLA Modules:
  0.0 33.1 jit_solution(12862419453790349306)
XLA Ops:
  0.6 27.3 %shard_map.113 = (f32[16,16,256]{2,1,0:T(8,128)}, f32[8,16,256]{2,1,0:T(8,128)}, bf16[256,256]{1,0:T(8,128)(2,1)}) custom-call(s32[16]{0:T(128)} %level_hbm.1, bf16[256,256]{1,0:T(8,128)(2,1)} %lat_hbm.1, bf16[256,256]{1,0:T(8,128)(2,1)} %lon_hbm.3, bf16[1,256,256]{2,1,0:T(8,128)(2,1)} %perts_hbm.3, f32[1,256,256]{2,1,0:T(8,128)} %control_hbm.3, ...), custom_call_target="tpu_custom_call" | custom-call | tf_op jit(solution)/shard_map/pallas_call | solution.py:537
  27.9 5.2 %shard_map.114 = (f32[1,256,256]{2,1,0:T(8,128)}, f32[8,16,256]{2,1,0:T(8,128)}) custom-call(f32[16,16,256]{2,1,0:T(8,128)} %get-tuple-element.5.grad_hbm, bf16[256,256]{1,0:T(8,128)(2,1)} %get-tuple-element.6.lat_hbm, bf16[256,256]{1,0:T(8,128)(2,1)} %lon_hbm.3, bf16[1,256,256]{2,1,0:T(8,128)(2,1)} %perts_hbm.3, f32[1,256,256]{2,1,0:T(8,128)} %control_hbm.3, ...), custom_call_target="tpu_custom_call" | custom-call | tf_op jit(solution)/shard_map/pallas_call | solution.py:593

commit v5 on v4

--- a/solution.py
+++ b/solution.py
@@ -153,8 +153,6 @@
     weighted,
     early_send,
     early_recv,
-    mid_send,
-    mid_recv,
     late_send,
     late_recv,
     grad,
@@ -166,8 +164,6 @@
     member_recv_sem,
     early_send_sem,
     early_recv_sem,
-    mid_send_sem,
-    mid_recv_sem,
     late_send_sem,
     late_recv_sem,
     grad_send_sem,
@@ -226,19 +222,21 @@
         smoothed, lon[...], (((1,), (1,)), ((), ())), preferred_element_type=jnp.float32
     )
     loads["perts"].wait()
-    field[...] = perts[...].astype(jnp.float32) * member
+    field[0:SIDE, :] = jnp.zeros((SIDE, cols), jnp.float32)
+    field[SIDE + nlat : 2 * SIDE + nlat, :] = jnp.zeros((SIDE, cols), jnp.float32)
+    field[SIDE : SIDE + nlat, :] = perts[...].astype(jnp.float32) * member
 
     pl.semaphore_wait(barrier, n - 1)
 
-    def piece(tile):
-        return pl.ds(pl.multiple_of(tile * rows, 8), rows)
+    def window(tile):
+        return pl.ds(pl.multiple_of(tile * rows, 8), win)
 
     order = sorted(range(1, n), key=lambda d: abs(2 * d - n))
     member_copies = []
     for d in order:
         peer = lax.rem(me + d, n)
         copy = pltpu.make_async_remote_copy(
-            src_ref=field.at[piece(peer)],
+            src_ref=field.at[window(peer)],
             dst_ref=received.at[me],
             send_sem=member_send_sem.at[d],
             recv_sem=member_recv_sem.at[d],
@@ -247,7 +245,7 @@
         )
         copy.start()
         member_copies.append(copy)
-    received[me] = field[piece(me), :]
+    received[me] = field[window(me), :]
 
     loads["coefs"].wait()
     loads["static"].wait()
@@ -258,6 +256,11 @@
             early_send[0, level, 2 * k : 2 * k + 2, :] = coefs[k, level, rows - 2 : rows, :]
             early_send[1, level, 2 * k : 2 * k + 2, :] = coefs[k, level, 0:2, :]
             coef_win[k, level, main, :] = coefs[k, level]
+        value = scale[level] * static[level]
+        at = half * SIDE
+        early_send[0, levels + pair, at : at + SIDE, :] = value[rows - SIDE : rows]
+        early_send[1, levels + pair, at : at + SIDE, :] = value[0:SIDE]
+        total_win[level, main, :] = value
 
     each_level(early_rows)
 
@@ -291,7 +294,6 @@
         one(out).wait_send()
 
     early = (early_send, early_recv, early_send_sem, early_recv_sem)
-    mid = (mid_send, mid_recv, mid_send_sem, mid_recv_sem)
     late = (late_send, late_recv, late_send_sem, late_recv_sem)
     exchange(*early, start)
 
@@ -330,13 +332,11 @@
     @pl.when(me == 0)
     def _():
         early_recv[0] = jnp.zeros(early_recv.shape[1:], jnp.float32)
-        mid_recv[0] = jnp.zeros(mid_recv.shape[1:], jnp.float32)
         late_recv[0] = jnp.zeros(late_recv.shape[1:], jnp.float32)
 
     @pl.when(me == n - 1)
     def _():
         early_recv[1] = jnp.zeros(early_recv.shape[1:], jnp.float32)
-        mid_recv[1] = jnp.zeros(mid_recv.shape[1:], jnp.float32)
         late_recv[1] = jnp.zeros(late_recv.shape[1:], jnp.float32)
 
     def unpack_early(pair, half, level):
@@ -351,6 +351,9 @@
             coef_win[k, level, SIDE + rows + 2 : win, :] = jnp.full(
                 (SIDE - 2, cols), 1.0 if k == 1 else 0.0, jnp.float32
             )
+        at = half * SIDE
+        total_win[level, 0:SIDE, :] = early_recv[0, levels + pair, at : at + SIDE, :]
+        total_win[level, SIDE + rows : win, :] = early_recv[1, levels + pair, at : at + SIDE, :]
         keep_win[level] = 1.0 - (
             coef_win[0, level] + coef_win[1, level] + coef_win[2, level] + coef_win[3, level]
         )
@@ -360,30 +363,17 @@
     for copy in member_copies:
         copy.wait_recv()
 
-    def add_up(pair, half, level):
-        total = scale[level] * static[level] + (
-            received[blocks_of[0, level]] + received[blocks_of[1, level]]
-        )
-        at = half * SIDE
-        mid_send[0, pair, at : at + SIDE, :] = total[rows - SIDE : rows]
-        mid_send[1, pair, at : at + SIDE, :] = total[0:SIDE]
-        total_win[level, main, :] = total
-
-    each_level(add_up, after=lambda pair: exchange(*mid, start, pair, 1))
-
     def forward(pair, half, level):
-        at = half * SIDE
-        total_win[level, 0:SIDE, :] = mid_recv[0, pair, at : at + SIDE, :]
-        total_win[level, SIDE + rows : win, :] = mid_recv[1, pair, at : at + SIDE, :]
-        state = total_win[level]
+        state = total_win[level] + (received[blocks_of[0, level]] + received[blocks_of[1, level]])
         c = [coef_win[k, level] for k in range(4)]
+        keep = keep_win[level]
         for k in range(STEPS):
             state = (
-                state
-                + c[0] * (pltpu.roll(state, win - 1, 0) - state)
-                + c[1] * (pltpu.roll(state, 1, 0) - state)
-                + c[2] * (pltpu.roll(state, cols - 1, 1) - state)
-                + c[3] * (pltpu.roll(state, 1, 1) - state)
+                keep * state
+                + c[0] * pltpu.roll(state, win - 1, 0)
+                + c[1] * pltpu.roll(state, 1, 0)
+                + c[2] * pltpu.roll(state, cols - 1, 1)
+                + c[3] * pltpu.roll(state, 1, 1)
             )
             value = weight_win[k, level] * (state - innov_win[k, level])
             weighted[k, level] = value
@@ -398,7 +388,6 @@
 
     each_level(
         forward,
-        before=lambda pair: exchange(*mid, wait_recv, pair, 1),
         after=lambda pair: exchange(*late, start, pair, 2),
     )
 
@@ -457,7 +446,6 @@
     exchange(*early, wait_send)
 
     def sent(pair):
-        exchange(*mid, wait_send, pair, 1)
         exchange(*late, wait_send, pair, 2)
 
     each_level(lambda *_: None, before=sent)
@@ -485,6 +473,7 @@
     perts,
     control,
     ens_new,
+    static_new,
     in_sem,
     out_sem,
 ):
@@ -496,18 +485,20 @@
             (lat_hbm, lat_t),
             (lon_hbm, lon),
             (control_hbm.at[0], control),
+            (static_hbm, static_new),
         )
     ):
         loads.append(pltpu.make_async_copy(source, target, in_sem.at[place]))
         loads[-1].start()
-    static_store = pltpu.make_async_copy(static_hbm, static_out, out_sem.at[2])
-    static_store.start()
-    for load in loads:
-        load.wait()
+    loads[0].wait()
+    loads[1].wait()
     nlat, cols = control.shape
     grad_field = gradient[...].reshape(nlat, cols)
     weighted_grad = (perts[...].astype(jnp.float32) * grad_field).astype(jnp.bfloat16)
-    stores = []
+    for load in loads[2:]:
+        load.wait()
+    stores = [pltpu.make_async_copy(static_new, static_out, out_sem.at[2])]
+    stores[0].start()
     for part in range(2):
         here = slice(part * nlat // 2, (part + 1) * nlat // 2)
         adjoint_lat = jnp.dot(
@@ -521,7 +512,6 @@
         stores[-1].start()
     for store in stores:
         store.wait()
-    static_store.wait()
 
 
 def fused(n, *args):
@@ -556,18 +546,16 @@
             pltpu.VMEM((STEPS,) + fields, f32),
             pltpu.VMEM((STEPS,) + fields, f32),
             pltpu.VMEM(loc_lat.shape, bf16),
-            pltpu.VMEM((nlat, cols), f32),
-            pltpu.VMEM((n, rows, cols), f32),
+            pltpu.VMEM((nlat + 2 * SIDE, cols), f32),
+            pltpu.VMEM((n, win, cols), f32),
             pltpu.VMEM((4,) + windows, f32),
             pltpu.VMEM(windows, f32),
             pltpu.VMEM(windows, f32),
             pltpu.VMEM((STEPS,) + windows, f32),
             pltpu.VMEM((STEPS,) + windows, f32),
             pltpu.VMEM((STEPS,) + windows, f32),
-            pltpu.VMEM((2, levels, 8, cols), f32),
-            pltpu.VMEM((2, levels, 8, cols), f32),
-            pltpu.VMEM((2, levels // 2, 8, cols), f32),
-            pltpu.VMEM((2, levels // 2, 8, cols), f32),
+            pltpu.VMEM((2, levels + levels // 2, 8, cols), f32),
+            pltpu.VMEM((2, levels + levels // 2, 8, cols), f32),
             pltpu.VMEM((2, levels, 8, cols), f32),
             pltpu.VMEM((2, levels, 8, cols), f32),
             pltpu.VMEM(fields, f32),
@@ -579,8 +567,6 @@
             dma((n,)),
             dma((2, 1)),
             dma((2, 1)),
-            dma((2, levels // 2)),
-            dma((2, levels // 2)),
             dma((2, levels // 2)),
             dma((2, levels // 2)),
             dma((n,)),
@@ -605,7 +591,8 @@
             pltpu.VMEM((nlat, cols), bf16),
             pltpu.VMEM((nlat, cols), f32),
             pltpu.VMEM((nlat, cols), f32),
-            dma((5,)),
+            pltpu.VMEM(fields, f32),
+            dma((6,)),
             dma((3,)),
         ],
     )(grad_field, lat_t, loc_lon, ens_perts, ens_control, static_new)

time: 33.2 us -> 30.7 us (0.925)
  Pallas kernels: 32.4 us -> 29.9 us
    pallas_call x1, Pallas kernels: 5.15 us -> 2.31 us  [fused(): pl.pallas_call(finish_kernel, out_shape=(jax.ShapeDtypeStruct(ens_control...]
    pallas_call x1, Pallas kernels: 27.3 us -> 27.6 us  [fused(): pl.pallas_call(functools.partial(kernel, n), out_shape=(jax.ShapeDtypeStr...]
where the time goes in v5:
time: 30.7 us; the launch traced here: 30.6 us
  Pallas kernels  29.9 us (97%)
  between operations  0.64 us (2%)
    pallas_call x1, Pallas kernels, fused(): pl.pallas_call(functools.partial(kernel, n), out_shape=(jax.ShapeDtypeStr...  27.6 us
    pallas_call x1, Pallas kernels, fused(): pl.pallas_call(finish_kernel, out_shape=(jax.ShapeDtypeStruct(ens_control...  2.31 us

profile of v5, /device:TPU:0, one launch (start us, length us, event | category | flops | bytes accessed | tf_op | source)
XLA Modules:
  0.0 30.6 jit_solution(13589676056054174077)
XLA Ops:
  0.6 27.6 %shard_map.113 = (f32[16,16,256]{2,1,0:T(8,128)}, f32[8,16,256]{2,1,0:T(8,128)}, bf16[256,256]{1,0:T(8,128)(2,1)}) custom-call(s32[16]{0:T(128)} %level_hbm.1, bf16[256,256]{1,0:T(8,128)(2,1)} %lat_hbm.1, bf16[256,256]{1,0:T(8,128)(2,1)} %lon_hbm.3, bf16[1,256,256]{2,1,0:T(8,128)(2,1)} %perts_hbm.3, f32[1,256,256]{2,1,0:T(8,128)} %control_hbm.3, ...), custom_call_target="tpu_custom_call" | custom-call | tf_op jit(solution)/shard_map/pallas_call | solution.py:527
  28.3 2.3 %shard_map.114 = (f32[1,256,256]{2,1,0:T(8,128)}, f32[8,16,256]{2,1,0:T(8,128)}) custom-call(f32[16,16,256]{2,1,0:T(8,128)} %get-tuple-element.5.grad_hbm, bf16[256,256]{1,0:T(8,128)(2,1)} %get-tuple-element.6.lat_hbm, bf16[256,256]{1,0:T(8,128)(2,1)} %lon_hbm.3, bf16[1,256,256]{2,1,0:T(8,128)(2,1)} %perts_hbm.3, f32[1,256,256]{2,1,0:T(8,128)} %control_hbm.3, ...), custom_call_target="tpu_custom_call" | custom-call | tf_op jit(solution)/shard_map/pallas_call | solution.py:579

commit v6 on v5

--- a/solution.py
+++ b/solution.py
@@ -202,15 +202,17 @@
         )
     ):
         loads[name] = pltpu.make_async_copy(source, target, in_sem.at[place])
+    for name in ("control", "lat", "lon", "perts"):
         loads[name].start()
-    level_load = pltpu.make_async_copy(level_hbm, level_map, out_sem.at[2])
-    level_load.start()
-
     barrier = pltpu.get_barrier_semaphore()
     for d in range(1, n):
         pl.semaphore_signal(
             barrier, inc=1, device_id={"tile": lax.rem(me + d, n)}, device_id_type=MESH
         )
+    for name in ("coefs", "static", "scale", "weight", "innov"):
+        loads[name].start()
+    level_load = pltpu.make_async_copy(level_hbm, level_map, out_sem.at[2])
+    level_load.start()
 
     loads["control"].wait()
     loads["lat"].wait()
@@ -233,19 +235,22 @@
 
     order = sorted(range(1, n), key=lambda d: abs(2 * d - n))
     member_copies = []
-    for d in order:
-        peer = lax.rem(me + d, n)
-        copy = pltpu.make_async_remote_copy(
-            src_ref=field.at[window(peer)],
-            dst_ref=received.at[me],
-            send_sem=member_send_sem.at[d],
-            recv_sem=member_recv_sem.at[d],
-            device_id={"tile": peer},
-            device_id_type=MESH,
-        )
-        copy.start()
-        member_copies.append(copy)
-    received[me] = field[window(me), :]
+
+    def send_members(distances):
+        for d in distances:
+            peer = lax.rem(me + d, n)
+            copy = pltpu.make_async_remote_copy(
+                src_ref=field.at[window(peer)],
+                dst_ref=received.at[me],
+                send_sem=member_send_sem.at[d],
+                recv_sem=member_recv_sem.at[d],
+                device_id={"tile": peer},
+                device_id_type=MESH,
+            )
+            copy.start()
+            member_copies.append(copy)
+
+    send_members(order[: n // 2])
 
     loads["coefs"].wait()
     loads["static"].wait()
@@ -255,12 +260,10 @@
         for k in range(4):
             early_send[0, level, 2 * k : 2 * k + 2, :] = coefs[k, level, rows - 2 : rows, :]
             early_send[1, level, 2 * k : 2 * k + 2, :] = coefs[k, level, 0:2, :]
-            coef_win[k, level, main, :] = coefs[k, level]
         value = scale[level] * static[level]
         at = half * SIDE
         early_send[0, levels + pair, at : at + SIDE, :] = value[rows - SIDE : rows]
         early_send[1, levels + pair, at : at + SIDE, :] = value[0:SIDE]
-        total_win[level, main, :] = value
 
     each_level(early_rows)
 
@@ -296,6 +299,8 @@
     early = (early_send, early_recv, early_send_sem, early_recv_sem)
     late = (late_send, late_recv, late_send_sem, late_recv_sem)
     exchange(*early, start)
+    send_members(order[n // 2 :])
+    received[me] = field[window(me), :]
 
     lat_t[...] = lat[...].astype(jnp.float32).T.astype(jnp.bfloat16)
     lat_store = pltpu.make_async_copy(lat_t, lat_out, out_sem.at[1])
@@ -305,6 +310,9 @@
     edge = jnp.zeros((SIDE, cols), jnp.float32)
 
     def widen(pair, half, level):
+        for k in range(4):
+            coef_win[k, level, main, :] = coefs[k, level]
+        total_win[level, main, :] = scale[level] * static[level]
         for k in range(STEPS):
             for target, source in ((weight_win, weight), (innov_win, innov)):
                 target[k, level, 0:SIDE, :] = edge

time: 30.7 us -> 30.7 us (level)
  no operation moved by 1% of the time
where the time goes in v6:
time: 30.7 us; the launch traced here: 30.5 us
  Pallas kernels  29.9 us (97%)
  between operations  0.64 us (2%)
    pallas_call x1, Pallas kernels, fused(): pl.pallas_call(functools.partial(kernel, n), out_shape=(jax.ShapeDtypeStr...  27.6 us
    pallas_call x1, Pallas kernels, fused(): pl.pallas_call(finish_kernel, out_shape=(jax.ShapeDtypeStruct(ens_control...  2.31 us

profile of v6, /device:TPU:0, one launch (start us, length us, event | category | flops | bytes accessed | tf_op | source)
XLA Modules:
  0.0 30.5 jit_solution(4793487498672249572)
XLA Ops:
  0.6 27.6 %shard_map.113 = (f32[16,16,256]{2,1,0:T(8,128)}, f32[8,16,256]{2,1,0:T(8,128)}, bf16[256,256]{1,0:T(8,128)(2,1)}) custom-call(s32[16]{0:T(128)} %level_hbm.1, bf16[256,256]{1,0:T(8,128)(2,1)} %lat_hbm.1, bf16[256,256]{1,0:T(8,128)(2,1)} %lon_hbm.3, bf16[1,256,256]{2,1,0:T(8,128)(2,1)} %perts_hbm.3, f32[1,256,256]{2,1,0:T(8,128)} %control_hbm.3, ...), custom_call_target="tpu_custom_call" | custom-call | tf_op jit(solution)/shard_map/pallas_call | solution.py:535
  28.2 2.3 %shard_map.114 = (f32[1,256,256]{2,1,0:T(8,128)}, f32[8,16,256]{2,1,0:T(8,128)}) custom-call(f32[16,16,256]{2,1,0:T(8,128)} %get-tuple-element.5.grad_hbm, bf16[256,256]{1,0:T(8,128)(2,1)} %get-tuple-element.6.lat_hbm, bf16[256,256]{1,0:T(8,128)(2,1)} %lon_hbm.3, bf16[1,256,256]{2,1,0:T(8,128)(2,1)} %perts_hbm.3, f32[1,256,256]{2,1,0:T(8,128)} %control_hbm.3, ...), custom_call_target="tpu_custom_call" | custom-call | tf_op jit(solution)/shard_map/pallas_call | solution.py:587

commit v7 on v6

--- a/solution.py
+++ b/solution.py
@@ -175,17 +175,17 @@
     win = rows + 2 * SIDE
     main = slice(SIDE, SIDE + rows)
 
-    def each_level(body, before=None, after=None):
-        def two(pair, carry):
+    def each_level(body, before=None, after=None, width=2):
+        def some(chunk, carry):
             if before is not None:
-                before(pair)
-            for half in range(2):
-                body(pair, half, 2 * pair + half)
+                before(chunk)
+            for at in range(width):
+                body(chunk * (width // 2) + at // 2, at % 2, width * chunk + at)
             if after is not None:
-                after(pair)
+                after(chunk)
             return carry
 
-        lax.fori_loop(0, levels // 2, two, 0)
+        lax.fori_loop(0, levels // width, some, 0)
 
     loads = {}
     for place, (name, source, target) in enumerate(
@@ -396,7 +396,8 @@
 
     each_level(
         forward,
-        after=lambda pair: exchange(*late, start, pair, 2),
+        after=lambda chunk: exchange(*late, start, chunk, 4),
+        width=4,
     )
 
     def backward(pair, half, level):
@@ -425,7 +426,7 @@
                 adjoint = adjoint + weighted[k, level]
         grad[level] = adjoint[SIDE : SIDE + rows]
 
-    each_level(backward, before=lambda pair: exchange(*late, wait_recv, pair, 2))
+    each_level(backward, before=lambda chunk: exchange(*late, wait_recv, chunk, 4), width=4)
 
     grad_copies = []
     for d in order:
@@ -453,10 +454,10 @@
         copy.wait_send()
     exchange(*early, wait_send)
 
-    def sent(pair):
-        exchange(*late, wait_send, pair, 2)
-
-    each_level(lambda *_: None, before=sent)
+    def sent(chunk):
+        exchange(*late, wait_send, chunk, 4)
+
+    each_level(lambda *_: None, before=sent, width=4)
     for copy in grad_copies:
         copy.wait_recv()
     for copy in grad_copies:
@@ -575,8 +576,8 @@
             dma((n,)),
             dma((2, 1)),
             dma((2, 1)),
-            dma((2, levels // 2)),
-            dma((2, levels // 2)),
+            dma((2, levels // 4)),
+            dma((2, levels // 4)),
             dma((n,)),
             dma((n,)),
         ],
@@ -615,7 +616,7 @@
         and rows % 8 == 0
         and rows * n == ens_control.shape[1]
         and cols % 128 == 0
-        and levels % 2 == 0
+        and levels % 4 == 0
         and STEPS == 3
     )
     return fused(n, *args) if fits else local(*args)

time: 30.7 us -> 30.3 us (0.987)
  Pallas kernels: 29.9 us -> 29.4 us
    pallas_call x1, Pallas kernels: 27.6 us -> 27.1 us  [fused(): pl.pallas_call(functools.partial(kernel, n), out_shape=(jax.ShapeDtypeStr...]
where the time goes in v7:
time: 30.3 us; the launch traced here: 30.1 us
  Pallas kernels  29.4 us (97%)
  between operations  0.64 us (2%)
    pallas_call x1, Pallas kernels, fused(): pl.pallas_call(functools.partial(kernel, n), out_shape=(jax.ShapeDtypeStr...  27.1 us
    pallas_call x1, Pallas kernels, fused(): pl.pallas_call(finish_kernel, out_shape=(jax.ShapeDtypeStruct(ens_control...  2.31 us

profile of v7, /device:TPU:0, one launch (start us, length us, event | category | flops | bytes accessed | tf_op | source)
XLA Modules:
  0.0 30.1 jit_solution(14843235145165403468)
XLA Ops:
  0.6 27.1 %shard_map.113 = (f32[16,16,256]{2,1,0:T(8,128)}, f32[8,16,256]{2,1,0:T(8,128)}, bf16[256,256]{1,0:T(8,128)(2,1)}) custom-call(s32[16]{0:T(128)} %level_hbm.1, bf16[256,256]{1,0:T(8,128)(2,1)} %lat_hbm.1, bf16[256,256]{1,0:T(8,128)(2,1)} %lon_hbm.3, bf16[1,256,256]{2,1,0:T(8,128)(2,1)} %perts_hbm.3, f32[1,256,256]{2,1,0:T(8,128)} %control_hbm.3, ...), custom_call_target="tpu_custom_call" | custom-call | tf_op jit(solution)/shard_map/pallas_call | solution.py:536
  27.8 2.3 %shard_map.114 = (f32[1,256,256]{2,1,0:T(8,128)}, f32[8,16,256]{2,1,0:T(8,128)}) custom-call(f32[16,16,256]{2,1,0:T(8,128)} %get-tuple-element.5.grad_hbm, bf16[256,256]{1,0:T(8,128)(2,1)} %get-tuple-element.6.lat_hbm, bf16[256,256]{1,0:T(8,128)(2,1)} %lon_hbm.3, bf16[1,256,256]{2,1,0:T(8,128)(2,1)} %perts_hbm.3, f32[1,256,256]{2,1,0:T(8,128)} %control_hbm.3, ...), custom_call_target="tpu_custom_call" | custom-call | tf_op jit(solution)/shard_map/pallas_call | solution.py:588
